TPU v7x, 128 devices: a whole 4x4x4 slice. The times are simulated.
128 devices in a mesh: section: 2 (over core), dp: 16 (over x, y), heads: 4 (over z).
Axes of the slice: x: 4, y: 4, z: 4, core: 2. Of those that a mesh axis runs over, the one named last changes fastest.
Arguments:
- patches: bfloat16 [12544, 768], P('dp'), may hold values from -6 to 6
- mask_flags: int32 [64, 196], P('dp'), may hold values 0 or 1
- image_tags: int32 [64], P('dp'), may hold values from 0 to 7
- mask_token: float32 [768], replicated, may hold values from -6 to 6
- group_table: float32 [8, 768], replicated, may hold values from -3 to 3
- qkv_weight: float32 [2, 768, 3, 768], P('section', 'dp'), may hold values from -0.21875 to 0.21875
- query_value_bias: float32 [2, 2, 768], P('section'), may hold values from -3 to 3
- out_weight: float32 [2, 768, 768], P('section', None, 'dp'), may hold values from -0.625 to 0.625
- up_weight: float32 [2, 768, 3072], P('section', 'dp'), may hold values from -0.21875 to 0.21875
- hidden_bias: float32 [2, 3072], P('section'), may hold values from -3 to 3
- down_weight: float32 [2, 3072, 768], P('section', None, 'dp'), may hold values from -0.109375 to 0.109375
- norm_gains: float32 [2, 2, 768], P('section'), may hold values from 0.5 to 1.5
- norm_biases: float32 [2, 4, 768], P('section'), may hold values from -2 to 2
- cotangent: bfloat16 [12544, 768], P('dp'), may hold values from -6 to 6
Outputs:
- stream_ends: float32 [2, 12544, 768], P('section', 'dp')
- grad_qkv: float32 [2, 768, 3, 768], P('section', 'dp')
- grad_qv_bias: float32 [2, 2, 768], P('section')
- grad_out: float32 [2, 768, 768], P('section', None, 'dp')
- grad_up: float32 [2, 768, 3072], P('section', 'dp')
- grad_hidden_bias: float32 [2, 3072], P('section')
- grad_down: float32 [2, 3072, 768], P('section', None, 'dp')
- grad_gains: float32 [2, 2, 768], P('section')
- grad_biases: float32 [2, 4, 768], P('section')
- grad_token: float32 [768], P('section')
- grad_table: float32 [8, 768], P(None, 'section')
Inputs may be any that keep to these rules, and one draw needn't show every extreme that they name: `image_tags`: the dataset group of each image; micro-batch (group mod 2) sizes may differ from device to device. `mask_flags`: 1 marks a masked patch.
All inputs are finite; a program needn't handle non-finite values. No bound on the sum of `mask_flags` on one device may be relied on, other than what follows from the above.
Results may differ from a plain program's by a relative error of at most 0.013.
Values may be sent and summed in bfloat16 or wider, within the bound.
No kernel may reach another device: no remote copies, remote signals or barrier semaphores. Data moves between devices by JAX's collectives and lax.ppermute only.
A program may use at most 192 MiB of HBM per device.

v0:
```python
import functools

import jax
import jax.numpy as jnp
from jax import lax
from jax.experimental import pallas as pl
from jax.experimental.pallas import tpu as pltpu
from jax.sharding import PartitionSpec as P

D = 768
HD = 64
FF = 3072
PATCHES = 196
ROWS = 208
GROUPS = 8
HALF = D // 2
HALF_FF = FF // 2
PAIR = 2 * HD
STEPS = 3
CHUNK = HALF_FF // STEPS
FEED = 2 * HALF_FF
ATTN = 4 * HALF
LAYER = FEED + ATTN
GATHERED = LAYER + ATTN
JOINED = LAYER + FEED
QUARTER = HALF_FF // 4
SIDE = 4
BLOCK = D // SIDE**2
MESH = ("section", "dp", "heads")
SWAP = [(0, 1), (1, 0)]
LIMIT = 48 * 2**20
ALL = 60 * 2**20
SCALE = HD ** (-0.5)
epsilon = 1e-06
f32 = jnp.float32
low = jnp.bfloat16


def dot(left, right):
    return jnp.dot(left, right, preferred_element_type=f32)


def dot_t(left, right):
    return lax.dot_general(left, right, (((1,), (1,)), ((), ())), preferred_element_type=f32)


def t_dot(left, right):
    return lax.dot_general(left, right, (((0,), (0,)), ((), ())), preferred_element_type=f32)


def both(own, other):
    return own[...].astype(f32) + other[...].astype(f32)


def column_sum(value):
    return jnp.sum(value.astype(f32), axis=0, keepdims=True)


def stats(value):
    average = jnp.mean(value, axis=-1, keepdims=True)
    centred = value - average
    rate = lax.rsqrt(jnp.mean(centred * centred, axis=-1, keepdims=True) + epsilon)
    return centred * rate, rate


def norm_back(value, gain, grad):
    x, rate = stats(value)
    scaled = grad * gain
    inner = scaled - jnp.mean(scaled, axis=-1, keepdims=True)
    inner = inner - x * jnp.mean(scaled * x, axis=-1, keepdims=True)
    return rate * inner, column_sum(grad * x), column_sum(grad)


def gauss(value):
    return 0.5 + 0.5 * lax.erf(value * 0.7071067811865476), jnp.exp(value * value * -0.5) * 0.3989422804014327


def head_masks():
    left = lax.broadcasted_iota(jnp.int32, (ROWS, PAIR), 1) < HD
    nothing = jnp.zeros((ROWS, PAIR), low)
    return left, (lambda rows: jnp.where(left, rows, nothing), lambda rows: jnp.where(left, nothing, rows))


def raw_scores(key_rows, queries):
    scores = dot_t(key_rows, queries) * SCALE
    return jnp.where(lax.broadcasted_iota(jnp.int32, scores.shape, 0) < PATCHES, scores, -1e30)


def start_blocks(slots, blocks, joined, sem, start, size, outwards=False):
    def body(inner, carry):
        for outer in range(SIDE):
            for half in range(2):
                i, j = (outer, inner) if outwards == (half == 0) else (inner, outer)
                row = pl.multiple_of(slots[i] * (SIDE * BLOCK) + slots[SIDE + j] * BLOCK, 16)
                ends = (
                    blocks[2 * half + outer // 2].at[outer % 2, inner, :, pl.ds(start, size)],
                    joined.at[pl.ds(row, BLOCK), pl.ds(half * size, size)],
                )
                pltpu.make_async_copy(*(reversed(ends) if outwards else ends), sem).start()
        return carry

    lax.fori_loop(0, SIDE, body, 0)


def all_landed(joined, sem):
    pltpu.make_async_copy(joined, joined, sem).wait()


def start_all(copies):
    for copy in copies:
        copy.start()


def wait_all(copies):
    for copy in copies:
        copy.wait()


def column_copies(whole, parts, sems, start, size, outwards=False):
    copies = []
    for k in range(parts.shape[0]):
        at = start[k] if isinstance(start, list) else start + k * size
        ends = whole.at[:, pl.ds(at, size)], parts.at[k]
        copies.append(pltpu.make_async_copy(*(reversed(ends) if outwards else ends), sems.at[k]))
    return copies


def column_copy(whole, parts, sems, start, size, k, outwards=False):
    ends = whole.at[:, pl.ds(pl.multiple_of(start + k * size, 128), size)], parts.at[k]
    return pltpu.make_async_copy(*(reversed(ends) if outwards else ends), sems.at[k])


def pair_forward(packed, write_lse):
    left, choose = head_masks()
    queries, keys, values = (packed[:, k * PAIR : (k + 1) * PAIR] for k in range(3))
    found = []
    for head in range(2):
        scores = raw_scores(keys, choose[head](queries))
        summit = jnp.max(scores, axis=0, keepdims=True)
        raised = jnp.exp(scores - summit)
        whole = jnp.sum(raised, axis=0, keepdims=True)
        write_lse(head, summit + jnp.log(whole))
        found.append(t_dot((raised * (1.0 / whole)).astype(low), values))
    return jnp.where(left, found[0], found[1]).astype(low)


def pair_backward(packed, lse, grad_pair, grad_packed):
    left, choose = head_masks()
    queries, keys, values = (packed[:, k * PAIR : (k + 1) * PAIR] for k in range(3))
    found = []
    for head in range(2):
        soft = jnp.exp(raw_scores(keys, choose[head](queries)) - lse[head : head + 1, :])
        grad_probs = dot_t(values, choose[head](grad_pair))
        within = jnp.sum(grad_probs * soft, axis=0, keepdims=True)
        grad_scores = (soft * (grad_probs - within)).astype(low)
        found.append((t_dot(grad_scores, keys) * SCALE, dot(grad_scores, queries) * SCALE, dot(soft.astype(low), grad_pair)))
    for k in range(3):
        grad_packed[:, k * PAIR : (k + 1) * PAIR] = jnp.where(left, found[0][k], found[1][k]).astype(low)
    return grad_packed[...]


def attention_kernel(second, *refs):
    if second:
        base, own, other, last_bias, norms, offset, weights, stream_out, *refs = refs
    else:
        base, norms, offset, weights, *refs = refs
    normed_out, packed_out, lse_out, context_out, part_out, weight, sems = refs
    copies = column_copies(weights, weight, sems, FEED + (ATTN if second else 0), 4 * PAIR)
    start_all(copies)
    stream = base[...]
    if second:
        stream = (stream + (both(own, other) + last_bias[...])).astype(low).astype(f32)
        stream_out[...] = stream
    normed = (stats(stream)[0] * norms[0:1] + norms[2:3]).astype(low)
    normed_out[...] = normed
    total = 0.0
    for k in range(STEPS):
        copies[k].wait()
        at = slice(k * 3 * PAIR, (k + 1) * 3 * PAIR)
        packed = (dot(normed, weight[k, :, : 3 * PAIR]) + offset[:, at]).astype(low)
        packed_out[:, at] = packed

        def write_lse(head, row):
            lse_out[k, head : head + 1, :] = row

        context = pair_forward(packed, write_lse)
        context_out[:, k * PAIR : (k + 1) * PAIR] = context
        total = total + dot_t(context, weight[k, :, 3 * PAIR :])
    part_out[...] = total.astype(low)


def forward_kernel(
    stream, own, other, norms, bias, weights, middle_out, normed_out, upper_out, part_out, weight, kept, sems, out_sems
):
    copies = column_copies(weights, weight, sems, 0, 2 * CHUNK)
    start_all(copies)
    leaving = column_copies(upper_out, kept, out_sems, 0, CHUNK, True)
    middle = stream[...] + (both(own, other) + norms[3:4])
    middle_out[...] = middle
    normed = (stats(middle)[0] * norms[1:2] + norms[4:5]).astype(low)
    normed_out[...] = normed
    total = 0.0
    for k in range(STEPS):
        copies[k].wait()
        upper = dot(normed, weight[k, :, :CHUNK]) + bias[:, k * CHUNK : (k + 1) * CHUNK]
        kept[k] = upper
        leaving[k].start()
        hidden = (upper * gauss(upper)[0]).astype(low)
        total = total + dot_t(hidden, weight[k, :, CHUNK:])
    part_out[...] = total.astype(low)
    for copy in leaving:
        copy.wait()


def turn_kernel(
    slots, branch, stream, own, other, norms, bias, near, far,
    grads_out, middle_out, mixed_out, part_out, bias_out, rows_out, weight, grads, normed, total, mixed, sems, out_sems,
):
    for k in range(SIDE):
        start_blocks(slots, [(near, far)[k // 2].at[k % 2, p] for p in range(SIDE)], weight.at[k], sems.at[k], 0, QUARTER)
    middle = stream[...] + (both(own, other) + norms[3:4])
    middle_out[...] = middle
    normed[...] = (stats(middle)[0] * norms[1:2] + norms[4:5]).astype(low)
    rows_out[2:3] = column_sum(branch[...])
    total[...] = jnp.zeros_like(total)
    mixed[...] = jnp.zeros_like(mixed)

    def leaving(k):
        columns = pl.ds(pl.multiple_of(slots[2 * SIDE + k] * 2 * QUARTER, 256), 2 * QUARTER)
        return pltpu.make_async_copy(grads.at[k], grads_out.at[:, columns], out_sems.at[k])

    def body(k, carry):
        at = pl.ds(pl.multiple_of(slots[2 * SIDE + k] * QUARTER, 128), QUARTER)
        rows, normed_now = branch[...], normed[...]
        all_landed(weight.at[k], sems.at[k])
        upper = dot(normed_now, weight[k, :, :QUARTER]) + bias[:, at]
        share, density = gauss(upper)
        hidden = (upper * share).astype(low)
        grad_upper = (dot(rows, weight[k, :, QUARTER:]) * (share + upper * density)).astype(low)
        total[...] += dot_t(grad_upper, weight[k, :, :QUARTER])
        grads[k, :, :QUARTER] = t_dot(normed_now, grad_upper).astype(low)
        grads[k, :, QUARTER:] = t_dot(rows, hidden).astype(low)
        leaving(k).start()
        bias_out[:, at] = column_sum(grad_upper)
        mixed[...] += dot_t(hidden, weight[k, :, QUARTER:])
        return carry

    lax.fori_loop(0, SIDE, body, 0)
    part_out[...] = total[...].astype(low)
    mixed_out[...] = mixed[...].astype(low)
    for k in range(SIDE):
        leaving(k).wait()


def backward_kernel(
    grad, own, other, stream, gains, normed_in, uppers, weights, _,
    grads_out, part_out, bias_out, rows_out, branch, weight, upper, grads, sems, upper_sems, out_sems,
):
    copies = column_copies(weights, weight, sems, 0, 2 * CHUNK)
    entering = column_copies(uppers, upper, upper_sems, 0, CHUNK)
    for pair in zip(copies, entering):
        for copy in pair:
            copy.start()
    leaving = column_copies(grads_out, grads, out_sems, FEED, 2 * CHUNK, True)
    into, gain, shift = norm_back(stream[...], gains[0:1], both(own, other))
    rows = (grad[...] + into).astype(low)
    branch[...] = rows
    rows_out[0:1] = gain
    rows_out[1:2] = shift
    rows_out[2:3] = column_sum(rows)
    normed = normed_in[...]

    def body(k, total):
        column_copy(uppers, upper, upper_sems, 0, CHUNK, k).wait()
        column_copy(weights, weight, sems, 0, 2 * CHUNK, k).wait()
        upper_now = upper[k]
        share, density = gauss(upper_now)
        hidden = (upper_now * share).astype(low)
        grad_upper = (dot(rows, weight[k, :, CHUNK:]) * (share + upper_now * density)).astype(low)
        grads[k, :, :CHUNK] = t_dot(normed, grad_upper).astype(low)
        grads[k, :, CHUNK:] = t_dot(rows, hidden).astype(low)
        column_copy(grads_out, grads, out_sems, FEED, 2 * CHUNK, k, True).start()
        bias_out[:, pl.ds(pl.multiple_of(k * CHUNK, 128), CHUNK)] = column_sum(grad_upper)
        return total + dot_t(grad_upper, weight[k, :, :CHUNK])

    part_out[...] = lax.fori_loop(0, STEPS, body, jnp.zeros((ROWS, D), f32)).astype(low)
    for copy in leaving:
        copy.wait()


def attention_back_kernel(second, *refs):
    if not second:
        slots, *refs = refs
    branch, own, other, middle, norms, normed_in, packed, lse, context, weights, *refs = refs
    if second:
        _, grads_out, *refs = refs
    else:
        blocks, refs = refs[:SIDE], refs[SIDE:]
    middle_out, part_out, rows_out, packed_out, weight, grads, grad_packed, sems, out_sems = refs
    copies = column_copies(weights, weight, sems, FEED + (ATTN if second else 0), 4 * PAIR)
    start_all(copies)
    if second:
        leaving = column_copies(grads_out, grads, out_sems, 2 * FEED, 4 * PAIR, True)
    into, gain, shift = norm_back(middle[...], norms[1:2], both(own, other))
    grad_middle = branch[...].astype(f32) + into
    middle_out[...] = grad_middle
    attn = grad_middle.astype(low)
    rows_out[0:1] = gain
    rows_out[1:2] = shift
    rows_out[2:3] = column_sum(attn)
    normed = normed_in[...]

    def pair_step(k, total):
        here, at = pl.ds(pl.multiple_of(k * PAIR, PAIR), PAIR), pl.ds(pl.multiple_of(k * 3 * PAIR, PAIR), 3 * PAIR)
        grad_pair = dot(attn, weight[k, :, 3 * PAIR :]).astype(low)
        rows = pair_backward(packed[:, at], lse[k], grad_pair, grad_packed)
        grads[k, :, : 3 * PAIR] = t_dot(normed, rows).astype(low)
        grads[k, :, 3 * PAIR :] = t_dot(attn, context[:, here]).astype(low)
        packed_out[:, at] = column_sum(rows)
        return total + dot_t(rows, weight[k, :, : 3 * PAIR])

    def body(k, total):
        column_copy(weights, weight, sems, FEED + (ATTN if second else 0), 4 * PAIR, k).wait()
        total = pair_step(k, total)
        if second:
            column_copy(grads_out, grads, out_sems, 2 * FEED, 4 * PAIR, k, True).start()
        else:
            start_blocks(slots, blocks, grads.at[k], out_sems.at[k], pl.multiple_of(2 * k * PAIR, 2 * PAIR), 2 * PAIR, True)
        return total

    total = lax.fori_loop(0, STEPS, body, jnp.zeros((ROWS, D), f32))
    part_out[...] = total.astype(low)
    for k in range(STEPS):
        if second:
            leaving[k].wait()
        else:
            all_landed(grads.at[k], out_sems.at[k])


def last_kernel(
    core, grad_middle, own, other, stream, norms, masked, tag, middle, mixed, mixed_other, last_bias,
    rows_one, sums_one, turn_rows, bias_one, rows_zero, sums_zero, back_rows, bias_zero, rows_out, vectors_low_out, vectors_out,
):
    into, gain, shift = norm_back(stream[...], norms[0:1], both(own, other))
    grad_zero = grad_middle[...] + into
    hidden = masked[...] > 0.5
    final = middle[...] + (both(mixed, mixed_other) + last_bias[...])
    first = core[0] == 0
    rows_out[...] = jnp.where(first, jnp.where(hidden, 0.0, grad_zero), final).astype(low)
    for at, gain_one, shift_one, attn_rows, feed_rows, sums, bias in (
        (0, gain, shift, rows_zero, back_rows, sums_zero, bias_zero),
        (9, back_rows[0:1], back_rows[1:2], rows_one, turn_rows, sums_one, bias_one),
    ):
        for k, row in enumerate((gain_one, attn_rows[0:1], shift_one, attn_rows[2:3], attn_rows[1:2], feed_rows[2:3])):
            vectors_out[at + k : at + k + 1] = row
        for k in range(STEPS):
            for part in range(2):
                to = part * HALF + k * PAIR
                vectors_out[at + 6 : at + 7, to : to + PAIR] = sums[:, (3 * k + 2 * part) * PAIR : (3 * k + 2 * part + 1) * PAIR]
        for k in range(2):
            vectors_out[at + 7 + k : at + 8 + k] = bias[:, k * D : (k + 1) * D]
    vectors_out[18:19] = column_sum(jnp.where(hidden, grad_zero, 0.0))
    table = column_sum(grad_zero)
    for group in range(GROUPS):
        vectors_out[19 + group : 20 + group] = jnp.where(tag[0] == group, table, 0.0)
    vectors_out[27:32] = jnp.zeros((5, D), f32)
    vectors_low_out[...] = jnp.zeros((BLOCK, 2 * HALF), low)
    vectors_low_out[0:32, 0:D] = vectors_out[...].astype(low)


def ends_kernel(order, parts, out):
    for k in range(SIDE):
        out[k * PATCHES : (k + 1) * PATCHES] = parts[order[k]].astype(f32)[:PATCHES]


def feed_columns(layer):
    size = QUARTER if layer == 1 else CHUNK
    return [(2 * at, slice(at, at + size), size) for at in range(0, HALF_FF, size)]


def attn_columns():
    return [[FEED + (4 * k + c) * PAIR for c in range(4)] for k in range(STEPS)]


def shards_kernel(core, qkv, out, up, down, mine_out, sent_out):
    def fill(layer, half, target):
        for to, units, size in feed_columns(layer):
            units = slice(units.start + half * HALF_FF, units.stop + half * HALF_FF)
            target[:, to : to + size] = up[:, units].astype(low)
            target[:, to + size : to + 2 * size] = down[:, units].astype(low)
        for k, spots in enumerate(attn_columns()):
            at = slice(half * HALF + k * PAIR, half * HALF + (k + 1) * PAIR)
            for to, rows in zip(spots, (qkv[0, :, at], qkv[1, :, at], qkv[2, :, at], out[:, at])):
                target[:, to : to + PAIR] = rows.astype(low)

    for index in range(2):
        @pl.when(core[0] == index)
        def _():
            fill(index, index, mine_out)
            fill(index, 1 - index, sent_out)


def grads_kernel(
    core, first_half, second_half,
    qkv_out, out_out, up_out, down_out, qv_out, hidden_out, gains_out, biases_out, token_out, table_out,
):
    halves = first_half, second_half
    shared = first_half[:, LAYER : LAYER + D].astype(f32)

    def fill(layer, half, part):
        for at, units, size in feed_columns(layer):
            units = slice(units.start + half * HALF_FF, units.stop + half * HALF_FF)
            up_out[:, units] = part[:, at : at + size].astype(f32)
            down_out[:, units] = part[:, at + size : at + 2 * size].astype(f32)
        for k, spots in enumerate(attn_columns()):
            to = slice(half * HALF + k * PAIR, half * HALF + (k + 1) * PAIR)
            for c in range(3):
                qkv_out[c, :, to] = part[:, spots[c] : spots[c] + PAIR].astype(f32)
            out_out[:, to] = part[:, spots[3] : spots[3] + PAIR].astype(f32)

    for index in range(2):
        @pl.when(core[0] == index)
        def _():
            at = 9 * index
            gains_out[...] = shared[at : at + 2]
            biases_out[...] = shared[at + 2 : at + 6]
            token_out[...] = shared[18:19, index * HALF : (index + 1) * HALF]
            table_out[...] = shared[19 : 19 + GROUPS, index * HALF : (index + 1) * HALF]
            for h, half in enumerate(halves):
                fill(index, h, half)
                rows = half[:, LAYER : LAYER + D].astype(f32)
                for k in range(2):
                    qv_out[k : k + 1, h * HALF : (h + 1) * HALF] = rows[at + 6 : at + 7, k * HALF : (k + 1) * HALF]
                    hidden_out[:, h * HALF_FF + k * D : h * HALF_FF + (k + 1) * D] = rows[at + 7 + k : at + 8 + k]


def whole(array):
    return pl.BlockSpec(array.shape, lambda *_: (0,) * len(array.shape))


def shaped(shape, kind=f32):
    return jax.ShapeDtypeStruct(shape, kind)


def call(kernel, name, operands, outs, specs, micros, alias=None, scratch=(), limit=LIMIT):
    def spec(key, array):
        return specs.get(key) or whole(array)

    return pl.pallas_call(
        kernel,
        name=name,
        grid=(1,),
        in_specs=[spec(("in", k), a) for k, a in enumerate(operands)],
        out_specs=[spec(("out", k), a) for k, a in enumerate(outs)],
        out_shape=outs,
        scratch_shapes=scratch,
        input_output_aliases=alias or {},
        cost_estimate=pl.CostEstimate(flops=0, bytes_accessed=int(micros * 3.6e6), transcendentals=0),
        compiler_params=pltpu.CompilerParams(vmem_limit_bytes=limit),
    )(*operands)


SMALL = pl.BlockSpec(memory_space=pltpu.SMEM)
LEFT = pl.BlockSpec(memory_space=pl.ANY)


STREAM = shaped((ROWS, D))
STREAM_LOW = shaped((ROWS, D), low)


DMA = pltpu.SemaphoreType.DMA((STEPS,))
FEED_PARTS = pltpu.VMEM((STEPS, D, 2 * CHUNK), low)
ATTN_PARTS = pltpu.VMEM((STEPS, D, 4 * PAIR), low)
UPPER_PARTS = pltpu.VMEM((STEPS, ROWS, CHUNK), f32)
ATTN_KEPT = [STREAM_LOW, shaped((ROWS, 3 * HALF), low), shaped((STEPS, 8, ROWS)), shaped((ROWS, HALF), low), STREAM_LOW]
JOINED_GRADS = shaped((D, JOINED), low)


def attention_call(layer, entry, norms, offset, weights):
    second = layer == 1
    operands = (*entry, norms, offset, weights)
    return call(
        functools.partial(attention_kernel, second), f"attention_{layer}", operands, [STREAM, *ATTN_KEPT] if second else ATTN_KEPT,
        {("in", len(operands) - 1): LEFT}, 4, scratch=[ATTN_PARTS, DMA],
    )


def forward_call(stream, part, part_other, norms, bias_up, weights):
    return call(
        forward_kernel, "feed_0", (stream, part, part_other, norms, bias_up, weights),
        [STREAM, STREAM_LOW, shaped((ROWS, HALF_FF)), STREAM_LOW], {("in", 5): LEFT, ("out", 2): LEFT}, 4,
        scratch=[FEED_PARTS, UPPER_PARTS, DMA, DMA],
    )


def turn_call(slots, branch, stream, part, part_other, norms, bias_up, near, far):
    parts, sems = pltpu.VMEM((SIDE, D, 2 * QUARTER), low), pltpu.SemaphoreType.DMA((SIDE,))
    return call(
        turn_kernel, "feed_1", (slots, branch, stream, part, part_other, norms, bias_up, near, far),
        [JOINED_GRADS, STREAM, STREAM_LOW, STREAM_LOW, shaped((1, HALF_FF)), shaped((8, D))],
        {("in", 0): SMALL, ("in", 7): LEFT, ("in", 8): LEFT, ("out", 0): LEFT}, 9,
        scratch=[parts, parts, pltpu.VMEM((ROWS, D), low), *[pltpu.VMEM((ROWS, D), f32)] * 2, sems, sems],
    )


def backward_call(entry, normed, upper, weights, grads):
    return call(
        backward_kernel, "feed_back_0", (*entry, normed, upper, weights, grads),
        [JOINED_GRADS, STREAM_LOW, shaped((1, HALF_FF)), shaped((8, D)), STREAM_LOW],
        {("in", 6): LEFT, ("in", 7): LEFT, ("in", 8): LEFT, ("out", 0): LEFT}, 6, alias={8: 0},
        scratch=[FEED_PARTS, UPPER_PARTS, FEED_PARTS, DMA, DMA, DMA],
    )


def attention_back_call(layer, entry, branch, part, part_other, middle, norms, normed, packed, lse, context, weights, grads):
    second = layer == 1
    operands = (*entry, branch, part, part_other, middle, norms, normed, packed, lse, context, weights, *grads)
    outs = [JOINED_GRADS] if second else [shaped((2, SIDE, BLOCK, 2 * HALF), low)] * SIDE
    count, last = len(outs), len(operands) - 1
    specs = {("in", k): LEFT for k in ((last - 1, last) if second else (last,))}
    if not second:
        specs["in", 0] = SMALL
    specs.update({("out", k): LEFT for k in range(count)})
    made = call(
        functools.partial(attention_back_kernel, second), f"attention_back_{layer}", operands,
        [*outs, STREAM, STREAM_LOW, shaped((8, D)), shaped((1, 3 * HALF))], specs, 7, alias={last: 0} if second else None,
        scratch=[ATTN_PARTS, ATTN_PARTS, pltpu.VMEM((ROWS, 3 * PAIR), low), DMA, DMA],
    )
    return made[:count], made[count:]


def swap(value):
    return lax.ppermute(value, "section", SWAP)


def routes(axis, turn):
    pairs = []
    for place in range(2 * SIDE**3):
        spot = [place // SIDE**3, place // SIDE**2 % SIDE, place // SIDE % SIDE, place % SIDE]
        spot[axis + 1] ^= 1 if spot[0] == turn else 3
        pairs.append((place, ((spot[0] * SIDE + spot[1]) * SIDE + spot[2]) * SIDE + spot[3]))
    return pairs


def trade(value, axis, turn):
    return lax.ppermute(value, MESH, routes(axis, turn))


def add(*values):
    return functools.reduce(jnp.add, (v.astype(f32) for v in values)).astype(low)


def both_of(own, axis, turn):
    return jnp.stack([own, trade(own, axis, turn)])


def gather_first(own, axis):
    pair = both_of(own, axis, 0)
    return jnp.concatenate([pair, trade(pair, axis, 1)])


def gather_second(own, axis):
    pair = both_of(own, axis, 0)
    return pair, trade(pair, axis, 1)


def halves_of(kept, got):
    middle = kept.shape[0] // 2
    return add(kept[:middle], got[:middle]), add(kept[middle:], got[middle:])


tied = lax.optimization_barrier


def per_device(
    patches, mask_flags, image_tags, mask_token, group_table, qkv_weight, query_value_bias, out_weight,
    up_weight, hidden_bias, down_weight, norm_gains, norm_biases, cotangent,
):
    place = lax.axis_index("heads")
    core = lax.axis_index("section")
    first = core == 0

    x, y = lax.axis_index("dp") // SIDE, lax.axis_index("dp") % SIDE
    flips = jnp.where(first, jnp.array([0, 1, 3, 2], jnp.int32), jnp.array([0, 3, 1, 2], jnp.int32))
    slots = jnp.concatenate([x ^ flips, y ^ flips, place ^ flips])
    order = jnp.argmax((place ^ flips)[None, :] == jnp.arange(SIDE, dtype=jnp.int32)[:, None], axis=1).astype(jnp.int32)

    rows = qkv_weight.shape[1]
    mine, other = call(
        shards_kernel, "shards",
        (core.reshape(1), qkv_weight[0].transpose(1, 0, 2), out_weight[0].T, up_weight[0], down_weight[0].T),
        [shaped((rows, LAYER), low)] * 2, {("in", 0): SMALL}, 2, limit=ALL,
    )
    other = swap(other)
    zero, one = jnp.where(first, mine, other), jnp.where(first, other, mine)

    shard = jnp.concatenate([zero, one[:, FEED:]], axis=1)
    weights = lax.all_gather(shard, "dp", axis=0, tiled=True)
    quarter = lax.dynamic_slice_in_dim(one, place * 2 * QUARTER, 2 * QUARTER, 1)
    near = gather_first(quarter[:, :QUARTER], 0), gather_first(quarter[:, QUARTER:], 1)
    near = jnp.stack([*gather_second(near[0], 1), *gather_second(near[1], 0)])
    near = both_of(near, 2, 0)
    far = trade(near, 2, 1)
    later = (patches, mask_flags, image_tags, mask_token, group_table, cotangent, norm_gains, norm_biases, query_value_bias, hidden_bias)
    later, _ = tied((later, near))
    patches, mask_flags, image_tags, mask_token, group_table, cotangent, norm_gains, norm_biases, query_value_bias, hidden_bias = later

    def half_of(vector):
        return jnp.where(first, vector[..., : vector.shape[-1] // 2], vector[..., vector.shape[-1] // 2 :])

    vectors = lax.all_gather(
        jnp.concatenate([norm_gains[0], norm_biases[0], query_value_bias[0], hidden_bias[0].reshape(4, D)]),
        "section", axis=0,
    )
    norms, offsets, bias_ups = [], [], []
    for layer in range(2):
        v = vectors[layer]
        norms.append(jnp.pad(v[:6], ((0, 2), (0, 0))))
        query, value = half_of(v[6:8]).reshape(2, STEPS, PAIR)
        offsets.append(jnp.stack([query, jnp.zeros_like(query), value], axis=1).reshape(1, 3 * HALF))
        bias_ups.append(half_of(v[8:12].reshape(1, FF)))

    def own(rows_of):
        return lax.dynamic_slice_in_dim(rows_of, place * PATCHES, PATCHES, 0)

    def padded(value):
        return jnp.pad(value, ((0, ROWS - PATCHES), (0, 0)))

    masked = lax.dynamic_slice_in_dim(mask_flags, place, 1, 0).reshape(PATCHES, 1).astype(f32)
    tag = lax.dynamic_slice_in_dim(image_tags, place, 1, 0)
    onehot = (tag[:, None] == jnp.arange(GROUPS, dtype=jnp.int32)[None, :]).astype(f32)
    image_row = jnp.sum(onehot.T * group_table, axis=0, keepdims=True)
    stream_zero = padded(jnp.where(masked > 0, mask_token[None, :], own(patches).astype(f32)) + image_row)
    seed, masked = padded(own(cotangent)), padded(masked)

    normed, packed, lse, context, part = attention_call(0, (stream_zero,), norms[0], offsets[0], weights)
    middle, normed_two, upper, mixed = forward_call(stream_zero, part, swap(part), norms[0], bias_ups[0], weights)
    kept = (middle, norms[0], normed, packed, lse, context)
    stream_one, normed, packed, lse, context, part = attention_call(
        1, (middle, mixed, swap(mixed), norms[0][5:6]), norms[1], offsets[1], weights
    )
    grads, middle, mixed, part, bias_one, turn_rows = turn_call(
        slots, seed, stream_one, part, swap(part), norms[1], bias_ups[1], near, far
    )
    (grads,), (grad_middle, part, rows_one, sums_one) = attention_back_call(
        1, (), seed, part, swap(part), middle, norms[1], normed, packed, lse, context, weights, [grads]
    )
    grads, part, bias_zero, back_rows, branch = backward_call(
        (grad_middle, part, swap(part), stream_one, norms[1]), normed_two, upper, weights, grads
    )
    joined = lax.psum_scatter(grads, "dp", scatter_dimension=0, tiled=True)
    (zero, sent, zero_too, sent_too), (grad_middle, part, rows_zero, sums_zero) = attention_back_call(
        0, (slots,), branch, part, swap(part), *kept, weights, []
    )
    rows_out, vectors, _ = call(
        last_kernel, "last",
        (
            core.reshape(1), grad_middle, part, swap(part), stream_zero, norms[0], masked, tag, middle, mixed, swap(mixed),
            norms[1][5:6], rows_one, sums_one, turn_rows, bias_one, rows_zero, sums_zero, back_rows, bias_zero,
        ),
        [STREAM_LOW, shaped((BLOCK, D), low), shaped((32, D))], {("in", 0): SMALL, ("in", 7): SMALL}, 3, limit=ALL,
    )

    def trade_with(sent, vectors, axis, turn):
        got = trade(jnp.concatenate([sent.reshape(-1, BLOCK, D), vectors[None]]), axis, turn)
        return got[:-1].reshape(sent.shape), add(vectors, got[-1])

    (got, vectors), got_too = trade_with(sent, vectors, 0, 1), trade(sent_too, 1, 1)
    got, got_too, rows_out = tied((got, got_too, rows_out))
    ends = both_of(rows_out, 2, 0)
    (zero, sent), (zero_too, sent_too) = halves_of(zero, got), halves_of(zero_too, got_too)
    (got, vectors), got_too = trade_with(sent, vectors, 0, 0), trade(sent_too, 1, 0)
    got, got_too, ends = tied((got, got_too, ends))
    ends = jnp.concatenate([ends, trade(ends, 2, 1)])
    (zero, sent), (zero_too, sent_too) = halves_of(zero[0], got[0]), halves_of(zero_too[0], got_too[0])
    (got, vectors), got_too = trade_with(sent, vectors, 1, 1), trade(sent_too, 0, 1)
    (zero, sent), (zero_too, sent_too) = halves_of(zero, got), halves_of(zero_too, got_too)
    (got, vectors), got_too = trade_with(sent, vectors, 1, 0), trade(sent_too, 0, 0)
    def by_pair(wide):
        return [wide[:, s * 2 * HALF + k * 2 * PAIR : s * 2 * HALF + (k + 1) * 2 * PAIR] for k in range(STEPS) for s in (0, 1)]

    attn_sum = jnp.concatenate([*by_pair(jnp.concatenate([add(zero[0], got[0]), add(zero_too[0], got_too[0])], axis=1)), vectors], axis=1)

    def z_sum(value):
        value = add(value, trade(value, 2, 0))
        return add(value, trade(value, 2, 1))

    attn_sum = z_sum(attn_sum)
    (ends_here,) = call(
        ends_kernel, "ends", (order, ends), [shaped((SIDE * PATCHES, D))], {("in", 0): SMALL}, 2
    )
    joined, attn_sum, ends_here = tied((joined, attn_sum, ends_here))

    joined = z_sum(joined)
    zero = jnp.concatenate([joined[:, FEED : 2 * FEED], attn_sum], axis=1)
    one = jnp.concatenate([joined[:, :FEED], joined[:, 2 * FEED :], attn_sum[:, ATTN:]], axis=1)
    mine = jnp.where(first, zero, one)
    other = swap(jnp.where(first, one, zero))
    grad_qkv, grad_out, grad_up, grad_down, grad_qv, grad_hidden, grad_gains, grad_biases, grad_token, grad_table = call(
        grads_kernel, "grads", (core.reshape(1), jnp.where(first, mine, other), jnp.where(first, other, mine)),
        [
            shaped((3, rows, D)), shaped((rows, D)), shaped((rows, FF)), shaped((rows, FF)), shaped((2, D)), shaped((1, FF)),
            shaped((2, D)), shaped((4, D)), shaped((1, HALF)), shaped((GROUPS, HALF)),
        ],
        {("in", 0): SMALL}, 2,
    )
    return (
        ends_here[None], grad_qkv.transpose(1, 0, 2)[None], grad_qv[None], grad_out.T[None], grad_up[None], grad_hidden,
        grad_down.T[None], grad_gains[None], grad_biases[None], grad_token[0], grad_table,
    )


def solution(mesh):
    in_specs = (
        P("dp", None), P("dp", None), P("dp"), P(), P(),
        P("section", "dp", None, None), P("section", None, None), P("section", None, "dp"),
        P("section", "dp", None), P("section", None), P("section", None, "dp"),
        P("section", None, None), P("section", None, None), P("dp", None),
    )
    out_specs = (
        P("section", "dp", None), P("section", "dp", None, None), P("section", None, None),
        P("section", None, "dp"), P("section", "dp", None), P("section", None), P("section", None, "dp"),
        P("section", None, None), P("section", None, None), P("section"), P(None, "section"),
    )
    return jax.shard_map(per_device, mesh=mesh, in_specs=in_specs, out_specs=out_specs, check_vma=False)
```

profile of v0, /device:TPU:1, one launch (start us, length us, event | category | flops | bytes accessed | tf_op | source)
XLA Modules:
  0.0 279.9 jit_solution(8227429399776612608)
XLA Ops:
  14.9 2.6 collective-permute-start.1
  17.5 2.7 collective-permute-start.5
  25.3 2.6 collective-permute-start.7
  29.3 3.4 %collective-permute-done.7 = bf16[4,48,384]{2,1,0:T(8,128)(2,1)S(1)} collective-permute-done((bf16[4,48,384]{2,1,0:T(8,128)(2,1)S(1)}, bf16[4,48,384]{2,1,0:T(8,128)(2,1)S(1)}, u32[]{:S(2)}, u32[]{:S(2)}) %collective-permute-start.7) | collective-permute-done | bytes 147488 | tf_op jit(solution)/shard_map/ppermute | solution.py:546
  32.9 7.0 %collective-permute-done.4 = bf16[2,4,48,384]{3,2,1,0:T(8,128)(2,1)S(1)} collective-permute-done((bf16[2,4,48,384]{3,2,1,0:T(8,128)(2,1)S(1)}, bf16[2,4,48,384]{3,2,1,0:T(8,128)(2,1)S(1)}, u32[]{:S(2)}, u32[]{:S(2)}) %collective-permute-start.4) | collective-permute-done | bytes 294944 | tf_op jit(solution)/shard_map/ppermute | solution.py:546
  39.9 4.7 %collective-permute-done.8 = bf16[2,4,48,384]{3,2,1,0:T(8,128)(2,1)S(1)} collective-permute-done((bf16[2,4,48,384]{3,2,1,0:T(8,128)(2,1)S(1)}, bf16[2,4,48,384]{3,2,1,0:T(8,128)(2,1)S(1)}, u32[]{:S(2)}, u32[]{:S(2)}) %collective-permute-start.8) | collective-permute-done | bytes 294944 | tf_op jit(solution)/shard_map/ppermute | solution.py:546
  45.9 2.7 collective-permute-start.9
  48.7 14.0 %collective-permute-done.9 = bf16[4,2,4,48,384]{4,3,2,1,0:T(8,128)(2,1)} collective-permute-done((bf16[4,2,4,48,384]{4,3,2,1,0:T(8,128)(2,1)}, bf16[4,2,4,48,384]{4,3,2,1,0:T(8,128)(2,1)}, u32[]{:S(2)}, u32[]{:S(2)}) %collective-permute-start.9) | collective-permute-done | bytes 1179680 | tf_op jit(solution)/shard_map/ppermute | solution.py:546
  62.8 3.0 %pad_maximum_fusion.near = bf16[2,4,2,4,48,384]{5,4,3,2,1,0:T(8,128)(2,1)} fusion(bf16[1,4,2,4,48,384]{5,4,3,2,1,0:T(8,128)(2,1)} %bitcast.21, bf16[1,4,2,4,48,384]{5,4,3,2,1,0:T(8,128)(2,1)S(1)} %get-tuple-element.167), kind=kLoop, calls=%fused_computation | loop fusion | flops 1179648 | bytes 4718592 | tf_op jit(solution)/shard_map/stack | solution.py:554
  67.2 6.6 %all-gather.1 = f32[2,12,768]{2,1,0:T(8,128)S(1)} all-gather(f32[1,12,768]{2,1,0:T(8,128)S(1)} %maximum_bitcast_fusion), channel_id=2, replica_groups=mesh['section'=2,'dp'=16,'heads'=4] {'section'}, dimensions={0}, use_global_device_ids=true | all-gather | bytes 110592 | tf_op jit(solution)/shard_map/all_gather | solution.py:611
  76.6 18.8 %all-gather.4.cloned.1.call-done.refs_3_.weights.refs_6_.refs_9_.refs_10_ = bf16[768,6144]{1,0:T(8,128)(2,1)} async-done(((bf16[48,6144]{1,0:T(8,128)(2,1)}), bf16[768,6144]{1,0:T(8,128)(2,1)}) %all-gather.4.cloned.1.call-update) | async-done | bytes 9437200 | tf_op jit(solution)/shard_map/all_gather | solution.py:598
  95.3 4.1 %attention_0.1 = (bf16[208,768]{1,0:T(8,128)(2,1)S(1)}, bf16[208,1152]{1,0:T(8,128)(2,1)S(1)}, f32[3,8,208]{2,1,0:T(8,128)S(1)}, bf16[208,384]{1,0:T(8,128)(2,1)S(1)}, bf16[208,768]{1,0:T(8,128)(2,1)S(1)}) custom-call(f32[208,768]{1,0:T(8,128)S(1)} %pad.20.refs_0_.stream, f32[8,768]{1,0:T(8,128)S(1)} %pad.21.refs_1_.norms.refs_5_, ...), custom_call_target="tpu_custom_call" | custom-call | bytes 14400000 | tf_op jit(solution)/shard_map/attention_0/pallas_call | solution.py:449
  102.1 4.2 %feed_0.1 = (f32[208,768]{1,0:T(8,128)S(1)}, bf16[208,768]{1,0:T(8,128)(2,1)S(1)}, f32[208,1536]{1,0:T(8,128)S(1)}, bf16[208,768]{1,0:T(8,128)(2,1)S(1)}) custom-call(f32[208,768]{1,0:T(8,128)S(1)} %pad.20.refs_0_.stream, bf16[208,768]{1,0:T(8,128)(2,1)S(1)} %get-tuple-element.96.own, bf16[208,768]{1,0:T(8,128)(2,1)S(1)} %collective-permute-done.10.other, ...), custom_call_target="tpu_custom_call" | custom-call | bytes 14400000 | tf_op jit(solution)/shard_map/feed_0/pallas_call | solution.py:449
  108.2 4.3 %attention_1.1 = (f32[208,768]{1,0:T(8,128)S(1)}, bf16[208,768]{1,0:T(8,128)(2,1)S(1)}, bf16[208,1152]{1,0:T(8,128)(2,1)S(1)}, f32[3,8,208]{2,1,0:T(8,128)S(1)},...) custom-call(f32[208,768]{1,0:T(8,128)S(1)} %get-tuple-element.97.refs_0_.refs_4_, ...), custom_call_target="tpu_custom_call" | custom-call | bytes 14400000 | tf_op jit(solution)/shard_map/attention_1/pallas_call | solution.py:449
  114.3 8.5 %feed_1.1 = (bf16[768,7680]{1,0:T(8,128)(2,1)}, f32[208,768]{1,0:T(8,128)S(1)}, bf16[208,768]{1,0:T(8,128)(2,1)S(1)}, bf16[208,768]{1,0:T(8,128)(2,1)S(1)}, f32[1,1536]{1,0:T(1,128)S(1)}, /*index=5*/f32[8,768]{1,0:T(8,128)S(1)}) custom-call(s32[12]{0:T(128)S(1)} %pad_add_fusion.slots.refs_0_, bf16[208,768]{1,0:T(8,128)(2,1)S(1)} %pad.19.branch.refs_0_, ...), custom_call_target="tpu_custom_call" | custom-call | bytes 32400000 | tf_op jit(solution)/shard_map/feed_1/pallas_call | solution.py:449
  125.0 7.4 %attention_back_1.1 = (bf16[768,7680]{1,0:T(8,128)(2,1)}, f32[208,768]{1,0:T(8,128)S(1)}, bf16[208,768]{1,0:T(8,128)(2,1)S(1)}, f32[8,768]{1,0:T(8,128)S(1)}, f32[1,1152]{1,0:T(1,128)S(1)}) custom-call(bf16[208,768]{1,0:T(8,128)(2,1)S(1)} %pad.19.branch.refs_0_, bf16[208,768]{1,0:T(8,128)(2,1)S(1)} %get-tuple-element.101.refs_1_, ...), custom_call_target="tpu_custom_call", output_to_operand_aliasing={{0}: (10, {})} | custom-call | bytes 25200000 | tf_op jit(solution)/shard_map/attention_back_1/pallas_call | solution.py:449
  134.6 6.3 %feed_back_0.1 = (bf16[768,7680]{1,0:T(8,128)(2,1)}, bf16[208,768]{1,0:T(8,128)(2,1)S(1)}, f32[1,1536]{1,0:T(1,128)S(1)}, f32[8,768]{1,0:T(8,128)S(1)}, bf16[208,768]{1,0:T(8,128)(2,1)S(1)}) custom-call(f32[208,768]{1,0:T(8,128)S(1)} %get-tuple-element.108.grad, bf16[208,768]{1,0:T(8,128)(2,1)S(1)} %get-tuple-element.109.own, ...), custom_call_target="tpu_custom_call", output_to_operand_aliasing={{0}: (8, {})} | custom-call | bytes 21600000 | tf_op jit(solution)/shard_map/feed_back_0/pallas_call | solution.py:449
  147.5 9.2 %attention_back_0.1 = (bf16[2,4,48,768]{3,2,1,0:T(8,128)(2,1)S(1)}, bf16[2,4,48,768]{3,2,1,0:T(8,128)(2,1)S(1)}, bf16[2,4,48,768]{3,2,1,0:T(8,128)(2,1)S(1)}, bf...) custom-call(s32[12]{0:T(128)S(1)} %pad_add_fusion.slots.refs_0_, ...), custom_call_target="tpu_custom_call" | custom-call | bytes 25200000 | tf_op jit(solution)/shard_map/attention_back_0/pallas_call | solution.py:449
  161.6 4.2 %last.1 = (bf16[208,768]{1,0:T(8,128)(2,1)}, bf16[48,768]{1,0:T(8,128)(2,1)}, f32[32,768]{1,0:T(8,128)}) custom-call(s32[1]{0:T(128)} %bitcast.core, f32[208,768]{1,0:T(8,128)} %copy-done.4, bf16[208,768]{1,0:T(8,128)(2,1)} %get-tuple-element.123.own, bf16[208,768]{1,0:T(8,128)(2,1)} %copy-done.25, f32[208,768]{1,0:T(8,128)} %copy-done.2, ...), custom_call_target="tpu_custom_call" | custom-call | bytes 10800000 | tf_op jit(solution)/shard_map/last/pallas_call | solution.py:449
  168.1 22.7 %collective-permute-done.19 = bf16[9,48,768]{2,1,0:T(8,128)(2,1)S(1)} collective-permute-done((bf16[9,48,768]{2,1,0:T(8,128)(2,1)S(1)}, bf16[9,48,768]{2,1,0:T(8,128)(2,1)S(1)}, u32[]{:S(2)}, u32[]{:S(2)}) %collective-permute-start.19) | collective-permute-done | bytes 663584 | tf_op jit(solution)/shard_map/ppermute | solution.py:546
  190.8 2.6 collective-permute-start.23
  193.6 2.7 collective-permute-start.21
  198.4 10.9 %collective-permute-done.21 = bf16[5,48,768]{2,1,0:T(8,128)(2,1)S(1)} collective-permute-done((bf16[5,48,768]{2,1,0:T(8,128)(2,1)S(1)}, bf16[5,48,768]{2,1,0:T(8,128)(2,1)S(1)}, u32[]{:S(2)}, u32[]{:S(2)}) %collective-permute-start.21) | collective-permute-done | bytes 368672 | tf_op jit(solution)/shard_map/ppermute | solution.py:546
  210.7 4.6 %collective-permute-done.26 = bf16[2,48,768]{2,1,0:T(8,128)(2,1)S(1)} collective-permute-done((bf16[2,48,768]{2,1,0:T(8,128)(2,1)S(1)}, bf16[2,48,768]{2,1,0:T(8,128)(2,1)S(1)}, u32[]{:S(2)}, u32[]{:S(2)}) %collective-permute-start.26) | collective-permute-done | bytes 147488 | tf_op jit(solution)/shard_map/ppermute | solution.py:546
  219.8 3.1 %collective-permute-done.25 = bf16[2,48,768]{2,1,0:T(8,128)(2,1)S(1)} collective-permute-done((bf16[2,48,768]{2,1,0:T(8,128)(2,1)S(1)}, bf16[2,48,768]{2,1,0:T(8,128)(2,1)S(1)}, u32[]{:S(2)}, u32[]{:S(2)}) %collective-permute-start.25) | collective-permute-done | bytes 147488 | tf_op jit(solution)/shard_map/ppermute | solution.py:546
  224.8 4.6 %collective-permute-done.28 = bf16[48,2304]{1,0:T(8,128)(2,1)S(1)} collective-permute-done((bf16[48,2304]{1,0:T(8,128)(2,1)S(1)}, bf16[48,2304]{1,0:T(8,128)(2,1)S(1)}, u32[]{:S(2)}, u32[]{:S(2)}) %collective-permute-start.28) | collective-permute-done | bytes 221216 | tf_op jit(solution)/shard_map/ppermute | solution.py:546
  230.2 6.6 %collective-permute-done.30 = bf16[2,208,768]{2,1,0:T(8,128)(2,1)S(1)} collective-permute-done((bf16[2,208,768]{2,1,0:T(8,128)(2,1)S(1)}, bf16[2,208,768]{2,1,0:T(8,128)(2,1)S(1)}, u32[]{:S(2)}, u32[]{:S(2)}) %collective-permute-start.30) | collective-permute-done | bytes 639008 | tf_op jit(solution)/shard_map/ppermute | solution.py:546
  239.3 3.0 %reduce-scatter.2.cloned.1.call-done = bf16[48,7680]{1,0:T(8,128)(2,1)} async-done(((bf16[768,7680]{1,0:T(8,128)(2,1)}), bf16[48,7680]{1,0:T(8,128)(2,1)}) %reduce-scatter.2.cloned.1.call-update) | async-done | bytes 737296 | tf_op jit(solution)/shard_map/reduce_scatter | solution.py:651
  242.2 2.7 collective-permute-start.31
  244.9 9.1 %collective-permute-done.31 = bf16[48,7680]{1,0:T(8,128)(2,1)S(1)} collective-permute-done((bf16[48,7680]{1,0:T(8,128)(2,1)}, bf16[48,7680]{1,0:T(8,128)(2,1)S(1)}, u32[]{:S(2)}, u32[]{:S(2)}) %collective-permute-start.31) | collective-permute-done | bytes 737312 | tf_op jit(solution)/shard_map/ppermute | solution.py:546
  255.7 10.3 %collective-permute-done.32 = bf16[48,7680]{1,0:T(8,128)(2,1)S(1)} collective-permute-done((bf16[48,7680]{1,0:T(8,128)(2,1)S(1)}, bf16[48,7680]{1,0:T(8,128)(2,1)S(1)}, u32[]{:S(2)}, u32[]{:S(2)}) %collective-permute-start.32) | collective-permute-done | bytes 737312 | tf_op jit(solution)/shard_map/ppermute | solution.py:546
  266.3 3.0 %collective-permute-start.33 = (bf16[48,5376]{1,0:T(8,128)(2,1)S(1)}, bf16[48,5376]{1,0:T(8,128)(2,1)S(1)}, u32[]{:S(2)}, u32[]{:S(2)}) collective-permute-start(bf16[48,5376]{1,0:T(8,128)(2,1)S(1)} %broadcast_select_fusion.2), channel_id=1, source_target_pairs={{0,64},{64,0},{1,65},{65,1},{2,66},{66,2},{3,67},{67,3},{4,68},{68... | collective-permute-start | bytes 1548296 | tf_op jit(solution)/shard_map/ppermute | solution.py:533
  (211 shorter events, 63.1 us)
Async XLA Ops:
  7.2 88.2 %all-gather.4.cloned.1.call-start = ((), (), s32[]{:S(2)}) async-start(), calls=%async_computation.1 | async-start | bytes 10027008 | tf_op jit(solution)/shard_map/all_gather | solution.py:598
  9.8 3.1 %collective-permute-start = (bf16[48,4608]{1,0:T(8,128)(2,1)}, bf16[48,4608]{1,0:T(8,128)(2,1)S(1)}, u32[]{:S(2)}, u32[]{:S(2)}) collective-permute-start(bf16[48,4608]{1,0:T(8,128)(2,1)} %get-tuple-element.84), channel_id=1, source_target_pairs={{0,64},{64,0},{1,65},{65,1},{2,66},{66,2},{3,67},{67,3},{4,68},{68... | collective-permute-start | bytes 1327112 | tf_op jit(solution)/shard_map/ppermute | solution.py:533
  14.8 227.4 %reduce-scatter.2.cloned.1.call-start = ((), (), s32[]{:S(2)}) async-start(), calls=%async_computation.2 | async-start | bytes 12533760 | tf_op jit(solution)/shard_map/reduce_scatter | solution.py:651
  14.9 5.4 %collective-permute-start.1 = (bf16[48,384]{1,0:T(8,128)(2,1)S(1)}, bf16[48,384]{1,0:T(8,128)(2,1)S(1)}, u32[]{:S(2)}, u32[]{:S(2)}) collective-permute-start(bf16[48,384]{1,0:T(8,128)(2,1)S(1)} %get-tuple-element.177), channel_id=1, source_target_pairs={{0,16},{1,17},{2,18},{3,19},{4,20},{5,21},{6,22},{7,23},{8,24},{9,... | collective-permute-start | bytes 110600 | tf_op jit(solution)/shard_map/ppermute | solution.py:546
  17.5 4.1 %collective-permute-start.5 = (bf16[48,384]{1,0:T(8,128)(2,1)S(1)}, bf16[48,384]{1,0:T(8,128)(2,1)S(1)}, u32[]{:S(2)}, u32[]{:S(2)}) collective-permute-start(bf16[48,384]{1,0:T(8,128)(2,1)S(1)} %get-tuple-element.178), channel_id=1, source_target_pairs={{0,4},{1,5},{2,6},{3,7},{4,0},{5,1},{6,2},{7,3},{8,12},{9,13},{10,... | collective-permute-start | bytes 110600 | tf_op jit(solution)/shard_map/ppermute | solution.py:546
  20.3 3.6 %collective-permute-start.2 = (bf16[2,48,384]{2,1,0:T(8,128)(2,1)S(1)}, bf16[2,48,384]{2,1,0:T(8,128)(2,1)S(1)}, u32[]{:S(2)}, u32[]{:S(2)}) collective-permute-start(bf16[2,48,384]{2,1,0:T(8,128)(2,1)S(1)} %pad_maximum_fusion.15), channel_id=1, source_target_pairs={{0,48},{1,49},{2,50},{3,51},{4,52},{5,53},{6,54},{7,55},{8,56},{9,... | collective-permute-start | bytes 221192 | tf_op jit(solution)/shard_map/ppermute | solution.py:546
  21.6 3.6 %collective-permute-start.6 = (bf16[2,48,384]{2,1,0:T(8,128)(2,1)S(1)}, bf16[2,48,384]{2,1,0:T(8,128)(2,1)S(1)}, u32[]{:S(2)}, u32[]{:S(2)}) collective-permute-start(bf16[2,48,384]{2,1,0:T(8,128)(2,1)S(1)} %pad_maximum_fusion.16), channel_id=1, source_target_pairs={{0,12},{1,13},{2,14},{3,15},{4,8},{5,9},{6,10},{7,11},{8,4},{9,5},... | collective-permute-start | bytes 221192 | tf_op jit(solution)/shard_map/ppermute | solution.py:546
  23.9 5.3 %collective-permute-start.3 = (bf16[4,48,384]{2,1,0:T(8,128)(2,1)S(1)}, bf16[4,48,384]{2,1,0:T(8,128)(2,1)S(1)}, u32[]{:S(2)}, u32[]{:S(2)}) collective-permute-start(bf16[4,48,384]{2,1,0:T(8,128)(2,1)S(1)} %get-tuple-element.184), channel_id=1, source_target_pairs={{0,4},{1,5},{2,6},{3,7},{4,0},{5,1},{6,2},{7,3},{8,12},{9,13},{10,... | collective-permute-start | bytes 442376 | tf_op jit(solution)/shard_map/ppermute | solution.py:546
  25.3 7.5 %collective-permute-start.7 = (bf16[4,48,384]{2,1,0:T(8,128)(2,1)S(1)}, bf16[4,48,384]{2,1,0:T(8,128)(2,1)S(1)}, u32[]{:S(2)}, u32[]{:S(2)}) collective-permute-start(bf16[4,48,384]{2,1,0:T(8,128)(2,1)S(1)} %get-tuple-element.186), channel_id=1, source_target_pairs={{0,16},{1,17},{2,18},{3,19},{4,20},{5,21},{6,22},{7,23},{8,24},{9,... | collective-permute-start | bytes 442376 | tf_op jit(solution)/shard_map/ppermute | solution.py:546
  29.2 10.7 %collective-permute-start.4 = (bf16[2,4,48,384]{3,2,1,0:T(8,128)(2,1)S(1)}, bf16[2,4,48,384]{3,2,1,0:T(8,128)(2,1)S(1)}, u32[]{:S(2)}, u32[]{:S(2)}) collective-permute-start(bf16[2,4,48,384]{3,2,1,0:T(8,128)(2,1)S(1)} %get-tuple-element.180), channel_id=1, source_target_pairs={{0,12},{1,13},{2,14},{3,15},{4,8},{5,9},{6,10},{7,11},{8,4},{9,5},... | collective-permute-start | bytes 884744 | tf_op jit(solution)/shard_map/ppermute | solution.py:546
  32.8 11.8 %collective-permute-start.8 = (bf16[2,4,48,384]{3,2,1,0:T(8,128)(2,1)S(1)}, bf16[2,4,48,384]{3,2,1,0:T(8,128)(2,1)S(1)}, u32[]{:S(2)}, u32[]{:S(2)}) collective-permute-start(bf16[2,4,48,384]{3,2,1,0:T(8,128)(2,1)S(1)} %get-tuple-element.182), channel_id=1, source_target_pairs={{0,48},{1,49},{2,50},{3,51},{4,52},{5,53},{6,54},{7,55},{8,56},{9,... | collective-permute-start | bytes 884744 | tf_op jit(solution)/shard_map/ppermute | solution.py:546
  45.9 16.9 %collective-permute-start.9 = (bf16[4,2,4,48,384]{4,3,2,1,0:T(8,128)(2,1)}, bf16[4,2,4,48,384]{4,3,2,1,0:T(8,128)(2,1)}, u32[]{:S(2)}, u32[]{:S(2)}) collective-permute-start(bf16[4,2,4,48,384]{4,3,2,1,0:T(8,128)(2,1)} %get-tuple-element.168), channel_id=1, source_target_pairs={{0,1},{1,0},{2,3},{3,2},{4,5},{5,4},{6,7},{7,6},{8,9},{9,8},{10,11... | collective-permute-start | bytes 3538952 | tf_op jit(solution)/shard_map/ppermute | solution.py:546
  65.8 47.2 %collective-permute-start.13 = (bf16[2,4,2,4,48,384]{5,4,3,2,1,0:T(8,128)(2,1)}, bf16[2,4,2,4,48,384]{5,4,3,2,1,0:T(8,128)(2,1)}, u32[]{:S(2)}, u32[]{:S(2)}) collective-permute-start(bf16[2,4,2,4,48,384]{5,4,3,2,1,0:T(8,128)(2,1)} %pad_maximum_fusion.near), channel_id=1, source_target_pairs={{0,3},{1,2},{2,1},{3,0},{4,7},{5,6},{6,5},{7,4},{8,11},{9,10},{10,... | collective-permute-start | bytes 7077896 | tf_op jit(solution)/shard_map/ppermute | solution.py:546
  100.2 1.9 collective-permute-start.10
  106.3 1.9 collective-permute-start.11
  143.3 16.8 %collective-permute-start.18 = (bf16[208,768]{1,0:T(8,128)(2,1)S(1)}, bf16[208,768]{1,0:T(8,128)(2,1)}, u32[]{:S(2)}, u32[]{:S(2)}) collective-permute-start(bf16[208,768]{1,0:T(8,128)(2,1)S(1)} %get-tuple-element.124.mixed), channel_id=1, source_target_pairs={{0,64},{64,0},{1,65},{65,1},{2,66},{66,2},{3,67},{67,3},{4,68},{68... | collective-permute-start | bytes 958472 | tf_op jit(solution)/shard_map/ppermute | solution.py:533
  159.0 1.8 collective-permute-start.17
  166.8 23.9 %collective-permute-start.19 = (bf16[9,48,768]{2,1,0:T(8,128)(2,1)S(1)}, bf16[9,48,768]{2,1,0:T(8,128)(2,1)S(1)}, u32[]{:S(2)}, u32[]{:S(2)}) collective-permute-start(bf16[9,48,768]{2,1,0:T(8,128)(2,1)S(1)} %pad_maximum_fusion.3), channel_id=1, source_target_pairs={{0,48},{1,49},{2,50},{3,51},{4,52},{5,53},{6,54},{7,55},{8,56},{9,... | collective-permute-start | bytes 1990664 | tf_op jit(solution)/shard_map/ppermute | solution.py:546
  168.0 22.8 %collective-permute-start.20 = (bf16[2,4,48,768]{3,2,1,0:T(8,128)(2,1)S(1)}, bf16[2,4,48,768]{3,2,1,0:T(8,128)(2,1)S(1)}, u32[]{:S(2)}, u32[]{:S(2)}) collective-permute-start(bf16[2,4,48,768]{3,2,1,0:T(8,128)(2,1)S(1)} %copy-done.22), channel_id=1, source_target_pairs={{0,12},{1,13},{2,14},{3,15},{4,8},{5,9},{6,10},{7,11},{8,4},{9,5},... | collective-permute-start | bytes 1769480 | tf_op jit(solution)/shard_map/ppermute | solution.py:546
  190.8 7.5 %collective-permute-start.23 = (bf16[208,768]{1,0:T(8,128)(2,1)S(1)}, bf16[208,768]{1,0:T(8,128)(2,1)S(1)}, u32[]{:S(2)}, u32[]{:S(2)}) collective-permute-start(bf16[208,768]{1,0:T(8,128)(2,1)S(1)} %copy-done.24), channel_id=1, source_target_pairs={{0,1},{1,0},{2,3},{3,2},{4,5},{5,4},{6,7},{7,6},{8,9},{9,8},{10,11... | collective-permute-start | bytes 958472 | tf_op jit(solution)/shard_map/ppermute | solution.py:546
  193.6 15.7 %collective-permute-start.21 = (bf16[5,48,768]{2,1,0:T(8,128)(2,1)S(1)}, bf16[5,48,768]{2,1,0:T(8,128)(2,1)S(1)}, u32[]{:S(2)}, u32[]{:S(2)}) collective-permute-start(bf16[5,48,768]{2,1,0:T(8,128)(2,1)S(1)} %pad_maximum_fusion.8), channel_id=1, source_target_pairs={{0,16},{1,17},{2,18},{3,19},{4,20},{5,21},{6,22},{7,23},{8,24},{9,... | collective-permute-start | bytes 1105928 | tf_op jit(solution)/shard_map/ppermute | solution.py:546
  196.4 13.2 %collective-permute-start.22 = (bf16[1,4,48,768]{3,2,1,0:T(8,128)(2,1)S(1)}, bf16[1,4,48,768]{3,2,1,0:T(8,128)(2,1)S(1)}, u32[]{:S(2)}, u32[]{:S(2)}) collective-permute-start(bf16[1,4,48,768]{3,2,1,0:T(8,128)(2,1)S(1)} %get-tuple-element.164), channel_id=1, source_target_pairs={{0,4},{1,5},{2,6},{3,7},{4,0},{5,1},{6,2},{7,3},{8,12},{9,13},{10,... | collective-permute-start | bytes 884744 | tf_op jit(solution)/shard_map/ppermute | solution.py:546
  209.6 5.6 %collective-permute-start.26 = (bf16[2,48,768]{2,1,0:T(8,128)(2,1)S(1)}, bf16[2,48,768]{2,1,0:T(8,128)(2,1)S(1)}, u32[]{:S(2)}, u32[]{:S(2)}) collective-permute-start(bf16[2,48,768]{2,1,0:T(8,128)(2,1)S(1)} %get-tuple-element.174), channel_id=1, source_target_pairs={{0,48},{1,49},{2,50},{3,51},{4,52},{5,53},{6,54},{7,55},{8,56},{9,... | collective-permute-start | bytes 442376 | tf_op jit(solution)/shard_map/ppermute | solution.py:546
  210.0 7.5 %collective-permute-start.24 = (bf16[3,48,768]{2,1,0:T(8,128)(2,1)S(1)}, bf16[3,48,768]{2,1,0:T(8,128)(2,1)S(1)}, u32[]{:S(2)}, u32[]{:S(2)}) collective-permute-start(bf16[3,48,768]{2,1,0:T(8,128)(2,1)S(1)} %pad_maximum_fusion.11), channel_id=1, source_target_pairs={{0,12},{1,13},{2,14},{3,15},{4,8},{5,9},{6,10},{7,11},{8,4},{9,5},... | collective-permute-start | bytes 663560 | tf_op jit(solution)/shard_map/ppermute | solution.py:546
  215.2 4.5 %collective-permute-start.27 = (bf16[1,48,768]{2,1,0:T(8,128)(2,1)S(1)}, bf16[1,48,768]{2,1,0:T(8,128)(2,1)S(1)}, u32[]{:S(2)}, u32[]{:S(2)}) collective-permute-start(bf16[1,48,768]{2,1,0:T(8,128)(2,1)S(1)} %fusion.4), channel_id=1, source_target_pairs={{0,16},{1,17},{2,18},{3,19},{4,20},{5,21},{6,22},{7,23},{8,24},{9,... | collective-permute-start | bytes 221192 | tf_op jit(solution)/shard_map/ppermute | solution.py:546
  217.6 5.3 %collective-permute-start.25 = (bf16[2,48,768]{2,1,0:T(8,128)(2,1)S(1)}, bf16[2,48,768]{2,1,0:T(8,128)(2,1)S(1)}, u32[]{:S(2)}, u32[]{:S(2)}) collective-permute-start(bf16[2,48,768]{2,1,0:T(8,128)(2,1)S(1)} %pad_maximum_fusion.14), channel_id=1, source_target_pairs={{0,4},{1,5},{2,6},{3,7},{4,0},{5,1},{6,2},{7,3},{8,12},{9,13},{10,... | collective-permute-start | bytes 442376 | tf_op jit(solution)/shard_map/ppermute | solution.py:546
  223.0 6.5 %collective-permute-start.28 = (bf16[48,2304]{1,0:T(8,128)(2,1)S(1)}, bf16[48,2304]{1,0:T(8,128)(2,1)S(1)}, u32[]{:S(2)}, u32[]{:S(2)}) collective-permute-start(bf16[48,2304]{1,0:T(8,128)(2,1)S(1)} %fusion.13), channel_id=1, source_target_pairs={{0,1},{1,0},{2,3},{3,2},{4,5},{5,4},{6,7},{7,6},{8,9},{9,8},{10,11... | collective-permute-start | bytes 663560 | tf_op jit(solution)/shard_map/ppermute | solution.py:546
  224.8 12.0 %collective-permute-start.30 = (bf16[2,208,768]{2,1,0:T(8,128)(2,1)S(1)}, bf16[2,208,768]{2,1,0:T(8,128)(2,1)S(1)}, u32[]{:S(2)}, u32[]{:S(2)}) collective-permute-start(bf16[2,208,768]{2,1,0:T(8,128)(2,1)S(1)} %pad_maximum_fusion.4), channel_id=1, source_target_pairs={{0,3},{1,2},{2,1},{3,0},{4,7},{5,6},{6,5},{7,4},{8,11},{9,10},{10,... | collective-permute-start | bytes 1916936 | tf_op jit(solution)/shard_map/ppermute | solution.py:546
  229.5 9.7 %collective-permute-start.29 = (bf16[48,2304]{1,0:T(8,128)(2,1)S(1)}, bf16[48,2304]{1,0:T(8,128)(2,1)S(1)}, u32[]{:S(2)}, u32[]{:S(2)}) collective-permute-start(bf16[48,2304]{1,0:T(8,128)(2,1)S(1)} %add_convert_fusion.7), channel_id=1, source_target_pairs={{0,3},{1,2},{2,1},{3,0},{4,7},{5,6},{6,5},{7,4},{8,11},{9,10},{10,... | collective-permute-start | bytes 663560 | tf_op jit(solution)/shard_map/ppermute | solution.py:546
  242.2 11.7 %collective-permute-start.31 = (bf16[48,7680]{1,0:T(8,128)(2,1)}, bf16[48,7680]{1,0:T(8,128)(2,1)S(1)}, u32[]{:S(2)}, u32[]{:S(2)}) collective-permute-start(bf16[48,7680]{1,0:T(8,128)(2,1)} %reduce-scatter.2.cloned.1.call-done), channel_id=1, source_target_pairs={{0,1},{1,0},{2,3},{3,2},{4,5},{5,4},{6,7},{7,6},{8,9},{9,8},{10,11... | collective-permute-start | bytes 2211848 | tf_op jit(solution)/shard_map/ppermute | solution.py:546
  255.3 10.7 %collective-permute-start.32 = (bf16[48,7680]{1,0:T(8,128)(2,1)S(1)}, bf16[48,7680]{1,0:T(8,128)(2,1)S(1)}, u32[]{:S(2)}, u32[]{:S(2)}) collective-permute-start(bf16[48,7680]{1,0:T(8,128)(2,1)S(1)} %add_convert_fusion.1), channel_id=1, source_target_pairs={{0,3},{1,2},{2,1},{3,0},{4,7},{5,6},{6,5},{7,4},{8,11},{9,10},{10,... | collective-permute-start | bytes 2211848 | tf_op jit(solution)/shard_map/ppermute | solution.py:546
  266.3 4.5 %collective-permute-start.33 = (bf16[48,5376]{1,0:T(8,128)(2,1)S(1)}, bf16[48,5376]{1,0:T(8,128)(2,1)S(1)}, u32[]{:S(2)}, u32[]{:S(2)}) collective-permute-start(bf16[48,5376]{1,0:T(8,128)(2,1)S(1)} %broadcast_select_fusion.2), channel_id=1, source_target_pairs={{0,64},{64,0},{1,65},{65,1},{2,66},{66,2},{3,67},{67,3},{4,68},{68... | collective-permute-start | bytes 1548296 | tf_op jit(solution)/shard_map/ppermute | solution.py:533
  (40 other events, 395.3 us)
Sparse Core Ops, SparseCore 0:
  14.9 80.3 all-gather.3
  142.4 99.7 reduce-scatter.1
where the time goes:
time: 280 us
  waiting for transfers between devices  141 us (50%)
  Pallas kernels  54.3 us (19%)
  starting transfers between devices  36.5 us (13%)
  between operations  14.8 us (5%)
  other arithmetic  14.1 us (5%)
  local copies, waits for them, and re-layouts  12.9 us (5%)
  blocking collectives  6.56 us (2%)
    ppermute x24, waiting for transfers between devices, trade(): return lax.ppermute(value, MESH, routes(axis, turn))  109 us
    pallas_call x11, Pallas kernels, call(): pl.pallas_call(kernel, name=name, grid=(1,), in_specs=[spec(('in', k), a)...  54.3 us
    ppermute x24, starting transfers between devices, trade(): return lax.ppermute(value, MESH, routes(axis, turn))  28.6 us
    all_gather x1, waiting for transfers between devices, per_device(): weights = lax.all_gather(shard, 'dp', axis=0, tiled=True)  18.8 us
    ppermute x10, waiting for transfers between devices, swap(): return lax.ppermute(value, 'section', SWAP)  10.4 us
    unnamed x81, local copies, waits for them, and re-layouts  9.93 us
    ppermute x10, starting transfers between devices, swap(): return lax.ppermute(value, 'section', SWAP)  7.78 us
    all_gather x1, blocking collectives, per_device(): lax.all_gather(jnp.concatenate([norm_gains[0], norm_biases[0], query_valu...  6.56 us
  transfers between devices with their start and end apart: 36, of which 30 were waited for; matrix products, arithmetic and copies ran while one was open for 5% of the time, Pallas kernels for 10%

commit v1 on v0

--- a/solution.py
+++ b/solution.py
@@ -102,6 +102,19 @@
     lax.fori_loop(0, SIDE, body, 0)
 
 
+def start_kinds(slots, outs, joined, sem, start):
+    def body(j, carry):
+        for k in range(SIDE):
+            kind = pl.ds(pl.multiple_of(slots[2 * SIDE + k] * PAIR, PAIR), PAIR)
+            for i in range(SIDE):
+                row = pl.multiple_of(slots[i] * (SIDE * BLOCK) + slots[SIDE + j] * BLOCK, 16)
+                there = outs[k // 2].at[k % 2, i // 2, i % 2, j, :, pl.ds(start, PAIR)]
+                pltpu.make_async_copy(joined.at[pl.ds(row, BLOCK), kind], there, sem).start()
+        return carry
+
+    lax.fori_loop(0, SIDE, body, 0)
+
+
 def all_landed(joined, sem):
     pltpu.make_async_copy(joined, joined, sem).wait()
 
@@ -295,7 +308,7 @@
     if second:
         _, grads_out, *refs = refs
     else:
-        blocks, refs = refs[:SIDE], refs[SIDE:]
+        kept_out, sent_out, *refs = refs
     middle_out, part_out, rows_out, packed_out, weight, grads, grad_packed, sems, out_sems = refs
     copies = column_copies(weights, weight, sems, FEED + (ATTN if second else 0), 4 * PAIR)
     start_all(copies)
@@ -325,7 +338,7 @@
         if second:
             column_copy(grads_out, grads, out_sems, 2 * FEED, 4 * PAIR, k, True).start()
         else:
-            start_blocks(slots, blocks, grads.at[k], out_sems.at[k], pl.multiple_of(2 * k * PAIR, 2 * PAIR), 2 * PAIR, True)
+            start_kinds(slots, (kept_out, sent_out), grads.at[k], out_sems.at[k], pl.multiple_of(k * PAIR, PAIR))
         return total
 
     total = lax.fori_loop(0, STEPS, body, jnp.zeros((ROWS, D), f32))
@@ -515,7 +528,7 @@
 def attention_back_call(layer, entry, branch, part, part_other, middle, norms, normed, packed, lse, context, weights, grads):
     second = layer == 1
     operands = (*entry, branch, part, part_other, middle, norms, normed, packed, lse, context, weights, *grads)
-    outs = [JOINED_GRADS] if second else [shaped((2, SIDE, BLOCK, 2 * HALF), low)] * SIDE
+    outs = [JOINED_GRADS] if second else [shaped((2, 2, 2, SIDE, BLOCK, HALF), low)] * 2
     count, last = len(outs), len(operands) - 1
     specs = {("in", k): LEFT for k in ((last - 1, last) if second else (last,))}
     if not second:
@@ -649,7 +662,7 @@
         (grad_middle, part, swap(part), stream_one, norms[1]), normed_two, upper, weights, grads
     )
     joined = lax.psum_scatter(grads, "dp", scatter_dimension=0, tiled=True)
-    (zero, sent, zero_too, sent_too), (grad_middle, part, rows_zero, sums_zero) = attention_back_call(
+    (kept, sent), (grad_middle, part, rows_zero, sums_zero) = attention_back_call(
         0, (slots,), branch, part, swap(part), *kept, weights, []
     )
     rows_out, vectors, _ = call(
@@ -662,38 +675,39 @@
     )
 
     def trade_with(sent, vectors, axis, turn):
-        got = trade(jnp.concatenate([sent.reshape(-1, BLOCK, D), vectors[None]]), axis, turn)
-        return got[:-1].reshape(sent.shape), add(vectors, got[-1])
-
-    (got, vectors), got_too = trade_with(sent, vectors, 0, 1), trade(sent_too, 1, 1)
-    got, got_too, rows_out = tied((got, got_too, rows_out))
+        got = trade(jnp.concatenate([sent.reshape(-1, BLOCK, HALF), vectors]), axis, turn)
+        return got[:-2].reshape(sent.shape), add(vectors, got[-2:])
+
+    vectors = jnp.stack([vectors[:, :HALF], vectors[:, HALF:]])
+    got, vectors = trade_with(sent, vectors, 2, 1)
+    kept, sent = halves_of(kept, got)
+    got, vectors = trade_with(sent, vectors, 2, 0)
+    kept, sent = add(kept[0], got[0])
+    sent, rows_out = tied((sent, rows_out))
+    got, vectors = trade_with(sent, vectors, 0, 1)
+    kept, sent = halves_of(kept, got)
+    got, vectors = trade_with(sent, vectors, 0, 0)
+    kept, sent = halves_of(kept[0], got[0])
     ends = both_of(rows_out, 2, 0)
-    (zero, sent), (zero_too, sent_too) = halves_of(zero, got), halves_of(zero_too, got_too)
-    (got, vectors), got_too = trade_with(sent, vectors, 0, 0), trade(sent_too, 1, 0)
-    got, got_too, ends = tied((got, got_too, ends))
     ends = jnp.concatenate([ends, trade(ends, 2, 1)])
-    (zero, sent), (zero_too, sent_too) = halves_of(zero[0], got[0]), halves_of(zero_too[0], got_too[0])
-    (got, vectors), got_too = trade_with(sent, vectors, 1, 1), trade(sent_too, 0, 1)
-    (zero, sent), (zero_too, sent_too) = halves_of(zero, got), halves_of(zero_too, got_too)
-    (got, vectors), got_too = trade_with(sent, vectors, 1, 0), trade(sent_too, 0, 0)
-    def by_pair(wide):
-        return [wide[:, s * 2 * HALF + k * 2 * PAIR : s * 2 * HALF + (k + 1) * 2 * PAIR] for k in range(STEPS) for s in (0, 1)]
-
-    attn_sum = jnp.concatenate([*by_pair(jnp.concatenate([add(zero[0], got[0]), add(zero_too[0], got_too[0])], axis=1)), vectors], axis=1)
-
-    def z_sum(value):
-        value = add(value, trade(value, 2, 0))
-        return add(value, trade(value, 2, 1))
-
-    attn_sum = z_sum(attn_sum)
+    got, vectors = trade_with(sent, vectors, 1, 1)
+    kept, sent = halves_of(kept, got)
+    got, vectors = trade_with(sent, vectors, 1, 0)
+    quarter = add(kept[0], got[0])
     (ends_here,) = call(
-        ends_kernel, "ends", (order, ends), [shaped((SIDE * PATCHES, D))], {("in", 0): SMALL}, 2
-    )
-    joined, attn_sum, ends_here = tied((joined, attn_sum, ends_here))
-
-    joined = z_sum(joined)
-    zero = jnp.concatenate([joined[:, FEED : 2 * FEED], attn_sum], axis=1)
-    one = jnp.concatenate([joined[:, :FEED], joined[:, 2 * FEED :], attn_sum[:, ATTN:]], axis=1)
+        ends_kernel, "ends", (order, ends), [shaped((SIDE * PATCHES, D))], {("in", 0): SMALL}, 2, limit=ALL
+    )
+    joined, quarter, vectors, ends_here = tied((joined, quarter, vectors, ends_here))
+
+    value = joined
+    for turn in range(2):
+        got = trade(jnp.concatenate([value, quarter], axis=1), 2, turn)
+        value, quarter = add(value, got[:, : value.shape[1]]), jnp.concatenate([quarter, got[:, value.shape[1] :]], axis=1)
+    quarter = quarter.reshape(rows, SIDE, HALF)
+    kinds = [lax.dynamic_index_in_dim(quarter, order[k], 1, keepdims=False) for k in range(SIDE)]
+    attn_zero = [kind[:, k * PAIR : (k + 1) * PAIR] for k in range(STEPS) for kind in kinds]
+    zero = jnp.concatenate([value[:, FEED : 2 * FEED], *attn_zero, vectors[0], vectors[1]], axis=1)
+    one = jnp.concatenate([value[:, :FEED], value[:, 2 * FEED :], vectors[0], vectors[1]], axis=1)
     mine = jnp.where(first, zero, one)
     other = swap(jnp.where(first, one, zero))
     grad_qkv, grad_out, grad_up, grad_down, grad_qv, grad_hidden, grad_gains, grad_biases, grad_token, grad_table = call(

time: 280 us -> 277 us (0.989)
  waiting for transfers between devices: 141 us -> 126 us
  between operations: 14.8 us -> 22.6 us
    ppermute x24 -> x20, waiting for transfers between devices: 109 us -> 90.6 us  [trade(): return lax.ppermute(value, MESH, routes(axis, turn))]
    reduce_scatter x1, waiting for transfers between devices: 2.97 us -> 6.23 us  [per_device(): joined = lax.psum_scatter(grads, 'dp', scatter_dimension=0, tiled=True)]
    ppermute x24 -> x20, starting transfers between devices: 28.6 us -> 28.1 us  [trade(): return lax.ppermute(value, MESH, routes(axis, turn))]
    unnamed x81 -> x96, local copies, waits for them, and re-layouts: 9.93 us -> 10.4 us
  transfers between devices with their start and end apart: 36 -> 32, of which waited for: 30 -> 28; matrix products, arithmetic and copies ran while one was open for 5% -> 5% of each run, Pallas kernels for 10% -> 11%
where the time goes in v1:
time: 277 us
  waiting for transfers between devices  126 us (45%)
  Pallas kernels  55.3 us (20%)
  starting transfers between devices  36.4 us (13%)
  between operations  22.6 us (8%)
  local copies, waits for them, and re-layouts  15.4 us (6%)
  other arithmetic  14.8 us (5%)
  blocking collectives  6.56 us (2%)
    ppermute x20, waiting for transfers between devices, trade(): return lax.ppermute(value, MESH, routes(axis, turn))  90.6 us
    pallas_call x11, Pallas kernels, call(): pl.pallas_call(kernel, name=name, grid=(1,), in_specs=[spec(('in', k), a)...  55.3 us
    ppermute x20, starting transfers between devices, trade(): return lax.ppermute(value, MESH, routes(axis, turn))  28.1 us
    all_gather x1, waiting for transfers between devices, per_device(): weights = lax.all_gather(shard, 'dp', axis=0, tiled=True)  18.6 us
    unnamed x96, local copies, waits for them, and re-layouts  10.4 us
    ppermute x10, waiting for transfers between devices, swap(): return lax.ppermute(value, 'section', SWAP)  10.3 us
    ppermute x10, starting transfers between devices, swap(): return lax.ppermute(value, 'section', SWAP)  8.24 us
    all_gather x1, blocking collectives, per_device(): lax.all_gather(jnp.concatenate([norm_gains[0], norm_biases[0], query_valu...  6.56 us
  transfers between devices with their start and end apart: 32, of which 28 were waited for; matrix products, arithmetic and copies ran while one was open for 5% of the time, Pallas kernels for 11%

profile of v1, /device:TPU:1, one launch (start us, length us, event | category | flops | bytes accessed | tf_op | source)
XLA Modules:
  0.0 276.8 jit_solution(2669268055075581987)
XLA Ops:
  7.2 2.5 shards.1
  14.9 2.6 collective-permute-start.1
  17.5 2.7 collective-permute-start.5
  25.3 2.6 collective-permute-start.7
  29.3 3.4 %collective-permute-done.7 = bf16[4,48,384]{2,1,0:T(8,128)(2,1)S(1)} collective-permute-done((bf16[4,48,384]{2,1,0:T(8,128)(2,1)S(1)}, bf16[4,48,384]{2,1,0:T(8,128)(2,1)S(1)}, u32[]{:S(2)}, u32[]{:S(2)}) %collective-permute-start.7) | collective-permute-done | bytes 147488 | tf_op jit(solution)/shard_map/ppermute | solution.py:559
  32.9 7.0 %collective-permute-done.4 = bf16[2,4,48,384]{3,2,1,0:T(8,128)(2,1)S(1)} collective-permute-done((bf16[2,4,48,384]{3,2,1,0:T(8,128)(2,1)S(1)}, bf16[2,4,48,384]{3,2,1,0:T(8,128)(2,1)S(1)}, u32[]{:S(2)}, u32[]{:S(2)}) %collective-permute-start.4) | collective-permute-done | bytes 294944 | tf_op jit(solution)/shard_map/ppermute | solution.py:559
  39.9 4.7 %collective-permute-done.8 = bf16[2,4,48,384]{3,2,1,0:T(8,128)(2,1)S(1)} collective-permute-done((bf16[2,4,48,384]{3,2,1,0:T(8,128)(2,1)S(1)}, bf16[2,4,48,384]{3,2,1,0:T(8,128)(2,1)S(1)}, u32[]{:S(2)}, u32[]{:S(2)}) %collective-permute-start.8) | collective-permute-done | bytes 294944 | tf_op jit(solution)/shard_map/ppermute | solution.py:559
  45.9 2.7 collective-permute-start.9
  48.7 14.0 %collective-permute-done.9 = bf16[4,2,4,48,384]{4,3,2,1,0:T(8,128)(2,1)} collective-permute-done((bf16[4,2,4,48,384]{4,3,2,1,0:T(8,128)(2,1)}, bf16[4,2,4,48,384]{4,3,2,1,0:T(8,128)(2,1)}, u32[]{:S(2)}, u32[]{:S(2)}) %collective-permute-start.9) | collective-permute-done | bytes 1179680 | tf_op jit(solution)/shard_map/ppermute | solution.py:559
  62.8 3.0 %pad_maximum_fusion.near = bf16[2,4,2,4,48,384]{5,4,3,2,1,0:T(8,128)(2,1)} fusion(bf16[1,4,2,4,48,384]{5,4,3,2,1,0:T(8,128)(2,1)} %bitcast.21, bf16[1,4,2,4,48,384]{5,4,3,2,1,0:T(8,128)(2,1)S(1)} %get-tuple-element.155), kind=kLoop, calls=%fused_computation | loop fusion | flops 1179648 | bytes 4718592 | tf_op jit(solution)/shard_map/stack | solution.py:567
  67.2 6.6 %all-gather.1 = f32[2,12,768]{2,1,0:T(8,128)S(1)} all-gather(f32[1,12,768]{2,1,0:T(8,128)S(1)} %maximum_bitcast_fusion), channel_id=2, replica_groups=mesh['section'=2,'dp'=16,'heads'=4] {'section'}, dimensions={0}, use_global_device_ids=true | all-gather | bytes 110592 | tf_op jit(solution)/shard_map/all_gather | solution.py:624
  76.8 18.6 %all-gather.4.cloned.1.call-done.refs_3_.weights.refs_6_.refs_9_.refs_10_ = bf16[768,6144]{1,0:T(8,128)(2,1)} async-done(((bf16[48,6144]{1,0:T(8,128)(2,1)}), bf16[768,6144]{1,0:T(8,128)(2,1)}) %all-gather.4.cloned.1.call-update) | async-done | bytes 9437200 | tf_op jit(solution)/shard_map/all_gather | solution.py:611
  95.3 4.1 %attention_0.1 = (bf16[208,768]{1,0:T(8,128)(2,1)S(1)}, bf16[208,1152]{1,0:T(8,128)(2,1)S(1)}, f32[3,8,208]{2,1,0:T(8,128)S(1)}, bf16[208,384]{1,0:T(8,128)(2,1)S(1)}, bf16[208,768]{1,0:T(8,128)(2,1)S(1)}) custom-call(f32[208,768]{1,0:T(8,128)S(1)} %pad.20.refs_0_.stream, f32[8,768]{1,0:T(8,128)S(1)} %pad.21.refs_1_.norms.refs_5_, ...), custom_call_target="tpu_custom_call" | custom-call | bytes 14400000 | tf_op jit(solution)/shard_map/attention_0/pallas_call | solution.py:462
  102.1 4.2 %feed_0.1 = (f32[208,768]{1,0:T(8,128)S(1)}, bf16[208,768]{1,0:T(8,128)(2,1)S(1)}, f32[208,1536]{1,0:T(8,128)S(1)}, bf16[208,768]{1,0:T(8,128)(2,1)S(1)}) custom-call(f32[208,768]{1,0:T(8,128)S(1)} %pad.20.refs_0_.stream, bf16[208,768]{1,0:T(8,128)(2,1)S(1)} %get-tuple-element.91.own, bf16[208,768]{1,0:T(8,128)(2,1)S(1)} %collective-permute-done.10.other, ...), custom_call_target="tpu_custom_call" | custom-call | bytes 14400000 | tf_op jit(solution)/shard_map/feed_0/pallas_call | solution.py:462
  108.2 4.3 %attention_1.1 = (f32[208,768]{1,0:T(8,128)S(1)}, bf16[208,768]{1,0:T(8,128)(2,1)S(1)}, bf16[208,1152]{1,0:T(8,128)(2,1)S(1)}, f32[3,8,208]{2,1,0:T(8,128)S(1)},...) custom-call(f32[208,768]{1,0:T(8,128)S(1)} %get-tuple-element.92.refs_0_.refs_4_, ...), custom_call_target="tpu_custom_call" | custom-call | bytes 14400000 | tf_op jit(solution)/shard_map/attention_1/pallas_call | solution.py:462
  114.3 8.4 %feed_1.1 = (bf16[768,7680]{1,0:T(8,128)(2,1)}, f32[208,768]{1,0:T(8,128)S(1)}, bf16[208,768]{1,0:T(8,128)(2,1)S(1)}, bf16[208,768]{1,0:T(8,128)(2,1)S(1)}, f32[1,1536]{1,0:T(1,128)S(1)}, /*index=5*/f32[8,768]{1,0:T(8,128)S(1)}) custom-call(s32[12]{0:T(128)S(1)} %pad_add_fusion.slots.refs_0_, bf16[208,768]{1,0:T(8,128)(2,1)S(1)} %pad.19.branch.refs_0_, ...), custom_call_target="tpu_custom_call" | custom-call | bytes 32400000 | tf_op jit(solution)/shard_map/feed_1/pallas_call | solution.py:462
  124.9 7.4 %attention_back_1.1 = (bf16[768,7680]{1,0:T(8,128)(2,1)}, f32[208,768]{1,0:T(8,128)S(1)}, bf16[208,768]{1,0:T(8,128)(2,1)S(1)}, f32[8,768]{1,0:T(8,128)S(1)}, f32[1,1152]{1,0:T(1,128)S(1)}) custom-call(bf16[208,768]{1,0:T(8,128)(2,1)S(1)} %pad.19.branch.refs_0_, bf16[208,768]{1,0:T(8,128)(2,1)S(1)} %get-tuple-element.96.refs_1_, ...), custom_call_target="tpu_custom_call", output_to_operand_aliasing={{0}: (10, {})} | custom-call | bytes 25200000 | tf_op jit(solution)/shard_map/attention_back_1/pallas_call | solution.py:462
  134.6 6.3 %feed_back_0.1 = (bf16[768,7680]{1,0:T(8,128)(2,1)}, bf16[208,768]{1,0:T(8,128)(2,1)S(1)}, f32[1,1536]{1,0:T(1,128)S(1)}, f32[8,768]{1,0:T(8,128)S(1)}, bf16[208,768]{1,0:T(8,128)(2,1)S(1)}) custom-call(f32[208,768]{1,0:T(8,128)S(1)} %get-tuple-element.103.grad, bf16[208,768]{1,0:T(8,128)(2,1)S(1)} %get-tuple-element.104.own, ...), custom_call_target="tpu_custom_call", output_to_operand_aliasing={{0}: (8, {})} | custom-call | bytes 21600000 | tf_op jit(solution)/shard_map/feed_back_0/pallas_call | solution.py:462
  147.1 9.4 %attention_back_0.1 = (bf16[2,2,2,4,48,384]{5,4,3,2,1,0:T(8,128)(2,1)S(1)}, bf16[2,2,2,4,48,384]{5,4,3,2,1,0:T(8,128)(2,1)S(1)}, f32[208,768]{1,0:T(8,128)S(1)},...) custom-call(s32[12]{0:T(128)S(1)} %pad_add_fusion.slots.refs_0_, ...), custom_call_target="tpu_custom_call" | custom-call | bytes 25200000 | tf_op jit(solution)/shard_map/attention_back_0/pallas_call | solution.py:462
  161.3 4.3 %last.1 = (bf16[208,768]{1,0:T(8,128)(2,1)}, bf16[48,768]{1,0:T(8,128)(2,1)}, f32[32,768]{1,0:T(8,128)}) custom-call(s32[1]{0:T(128)} %bitcast.core, f32[208,768]{1,0:T(8,128)} %copy-done.6, bf16[208,768]{1,0:T(8,128)(2,1)} %copy-done.9, bf16[208,768]{1,0:T(8,128)(2,1)} %copy-done.26, f32[208,768]{1,0:T(8,128)} %copy-done.2, f32[8,768]{1,0:T(8,128)} %copy-done.7, ...), custom_call_target="tpu_custom_call" | custom-call | bytes 10800000 | tf_op jit(solution)/shard_map/last/pallas_call | solution.py:462
  167.9 15.1 %collective-permute-done.19 = bf16[34,48,384]{2,1,0:T(8,128)(2,1)S(1)} collective-permute-done((bf16[34,48,384]{2,1,0:T(8,128)(2,1)S(1)}, bf16[34,48,384]{2,1,0:T(8,128)(2,1)S(1)}, u32[]{:S(2)}, u32[]{:S(2)}) %collective-permute-start.19) | collective-permute-done | bytes 1253408 | tf_op jit(solution)/shard_map/ppermute | solution.py:559
  183.3 2.7 collective-permute-start.20
  186.0 8.1 %collective-permute-done.20 = bf16[18,48,384]{2,1,0:T(8,128)(2,1)S(1)} collective-permute-done((bf16[18,48,384]{2,1,0:T(8,128)(2,1)S(1)}, bf16[18,48,384]{2,1,0:T(8,128)(2,1)S(1)}, u32[]{:S(2)}, u32[]{:S(2)}) %collective-permute-start.20) | collective-permute-done | bytes 663584 | tf_op jit(solution)/shard_map/ppermute | solution.py:559
  196.2 10.9 %collective-permute-done.21 = bf16[10,48,384]{2,1,0:T(8,128)(2,1)S(1)} collective-permute-done((bf16[10,48,384]{2,1,0:T(8,128)(2,1)S(1)}, bf16[10,48,384]{2,1,0:T(8,128)(2,1)S(1)}, u32[]{:S(2)}, u32[]{:S(2)}) %collective-permute-start.21) | collective-permute-done | bytes 368672 | tf_op jit(solution)/shard_map/ppermute | solution.py:559
  214.1 2.3 collective-permute-done.25
  220.4 5.5 %collective-permute-done.24 = bf16[3,48,384]{2,1,0:T(8,128)(2,1)S(1)} collective-permute-done((bf16[3,48,384]{2,1,0:T(8,128)(2,1)S(1)}, bf16[3,48,384]{2,1,0:T(8,128)(2,1)S(1)}, u32[]{:S(2)}, u32[]{:S(2)}) %collective-permute-start.24) | collective-permute-done | bytes 110624 | tf_op jit(solution)/shard_map/ppermute | solution.py:559
  227.5 3.0 %ends.1 = f32[784,768]{1,0:T(8,128)} custom-call(s32[4]{0:T(128)} %get-tuple-element.131.order, bf16[4,208,768]{2,1,0:T(8,128)(2,1)} %pad_maximum_fusion.1.parts), custom_call_target="tpu_custom_call" | custom-call | bytes 7200000 | tf_op jit(solution)/shard_map/ends/pallas_call | solution.py:462
  230.4 6.2 %reduce-scatter.2.cloned.1.call-done = bf16[48,7680]{1,0:T(8,128)(2,1)} async-done(((bf16[768,7680]{1,0:T(8,128)(2,1)}), bf16[48,7680]{1,0:T(8,128)(2,1)}) %reduce-scatter.2.cloned.1.call-update) | async-done | bytes 737296 | tf_op jit(solution)/shard_map/reduce_scatter | solution.py:664
  237.9 2.6 collective-permute-start.27
  240.5 9.4 %collective-permute-done.27 = bf16[48,8064]{1,0:T(8,128)(2,1)S(1)} collective-permute-done((bf16[48,8064]{1,0:T(8,128)(2,1)S(1)}, bf16[48,8064]{1,0:T(8,128)(2,1)S(1)}, u32[]{:S(2)}, u32[]{:S(2)}) %collective-permute-start.27) | collective-permute-done | bytes 774176 | tf_op jit(solution)/shard_map/ppermute | solution.py:559
  259.1 2.5 collective-permute-done.28
  262.7 3.5 %collective-permute-start.29 = (bf16[48,5376]{1,0:T(8,128)(2,1)S(1)}, bf16[48,5376]{1,0:T(8,128)(2,1)S(1)}, u32[]{:S(2)}, u32[]{:S(2)}) collective-permute-start(bf16[48,5376]{1,0:T(8,128)(2,1)S(1)} %broadcast_select_fusion.2), channel_id=1, source_target_pairs={{0,64},{64,0},{1,65},{65,1},{2,66},{66,2},{3,67},{67,3},{4,68},{68... | collective-permute-start | bytes 1548296 | tf_op jit(solution)/shard_map/ppermute | solution.py:546
  (228 shorter events, 63.4 us)
Async XLA Ops:
  7.2 88.2 %all-gather.4.cloned.1.call-start = ((), (), s32[]{:S(2)}) async-start(), calls=%async_computation.1 | async-start | bytes 10027008 | tf_op jit(solution)/shard_map/all_gather | solution.py:611
  9.8 3.1 %collective-permute-start = (bf16[48,4608]{1,0:T(8,128)(2,1)}, bf16[48,4608]{1,0:T(8,128)(2,1)S(1)}, u32[]{:S(2)}, u32[]{:S(2)}) collective-permute-start(bf16[48,4608]{1,0:T(8,128)(2,1)} %get-tuple-element.79), channel_id=1, source_target_pairs={{0,64},{64,0},{1,65},{65,1},{2,66},{66,2},{3,67},{67,3},{4,68},{68... | collective-permute-start | bytes 1327112 | tf_op jit(solution)/shard_map/ppermute | solution.py:546
  14.8 221.8 %reduce-scatter.2.cloned.1.call-start = ((), (), s32[]{:S(2)}) async-start(), calls=%async_computation.2 | async-start | bytes 12533760 | tf_op jit(solution)/shard_map/reduce_scatter | solution.py:664
  14.9 5.4 %collective-permute-start.1 = (bf16[48,384]{1,0:T(8,128)(2,1)S(1)}, bf16[48,384]{1,0:T(8,128)(2,1)S(1)}, u32[]{:S(2)}, u32[]{:S(2)}) collective-permute-start(bf16[48,384]{1,0:T(8,128)(2,1)S(1)} %get-tuple-element.163), channel_id=1, source_target_pairs={{0,16},{1,17},{2,18},{3,19},{4,20},{5,21},{6,22},{7,23},{8,24},{9,... | collective-permute-start | bytes 110600 | tf_op jit(solution)/shard_map/ppermute | solution.py:559
  17.5 4.1 %collective-permute-start.5 = (bf16[48,384]{1,0:T(8,128)(2,1)S(1)}, bf16[48,384]{1,0:T(8,128)(2,1)S(1)}, u32[]{:S(2)}, u32[]{:S(2)}) collective-permute-start(bf16[48,384]{1,0:T(8,128)(2,1)S(1)} %get-tuple-element.164), channel_id=1, source_target_pairs={{0,4},{1,5},{2,6},{3,7},{4,0},{5,1},{6,2},{7,3},{8,12},{9,13},{10,... | collective-permute-start | bytes 110600 | tf_op jit(solution)/shard_map/ppermute | solution.py:559
  20.3 3.6 %collective-permute-start.2 = (bf16[2,48,384]{2,1,0:T(8,128)(2,1)S(1)}, bf16[2,48,384]{2,1,0:T(8,128)(2,1)S(1)}, u32[]{:S(2)}, u32[]{:S(2)}) collective-permute-start(bf16[2,48,384]{2,1,0:T(8,128)(2,1)S(1)} %pad_maximum_fusion.19), channel_id=1, source_target_pairs={{0,48},{1,49},{2,50},{3,51},{4,52},{5,53},{6,54},{7,55},{8,56},{9,... | collective-permute-start | bytes 221192 | tf_op jit(solution)/shard_map/ppermute | solution.py:559
  21.6 3.6 %collective-permute-start.6 = (bf16[2,48,384]{2,1,0:T(8,128)(2,1)S(1)}, bf16[2,48,384]{2,1,0:T(8,128)(2,1)S(1)}, u32[]{:S(2)}, u32[]{:S(2)}) collective-permute-start(bf16[2,48,384]{2,1,0:T(8,128)(2,1)S(1)} %pad_maximum_fusion.20), channel_id=1, source_target_pairs={{0,12},{1,13},{2,14},{3,15},{4,8},{5,9},{6,10},{7,11},{8,4},{9,5},... | collective-permute-start | bytes 221192 | tf_op jit(solution)/shard_map/ppermute | solution.py:559
  23.9 5.3 %collective-permute-start.3 = (bf16[4,48,384]{2,1,0:T(8,128)(2,1)S(1)}, bf16[4,48,384]{2,1,0:T(8,128)(2,1)S(1)}, u32[]{:S(2)}, u32[]{:S(2)}) collective-permute-start(bf16[4,48,384]{2,1,0:T(8,128)(2,1)S(1)} %get-tuple-element.177), channel_id=1, source_target_pairs={{0,4},{1,5},{2,6},{3,7},{4,0},{5,1},{6,2},{7,3},{8,12},{9,13},{10,... | collective-permute-start | bytes 442376 | tf_op jit(solution)/shard_map/ppermute | solution.py:559
  25.3 7.5 %collective-permute-start.7 = (bf16[4,48,384]{2,1,0:T(8,128)(2,1)S(1)}, bf16[4,48,384]{2,1,0:T(8,128)(2,1)S(1)}, u32[]{:S(2)}, u32[]{:S(2)}) collective-permute-start(bf16[4,48,384]{2,1,0:T(8,128)(2,1)S(1)} %get-tuple-element.179), channel_id=1, source_target_pairs={{0,16},{1,17},{2,18},{3,19},{4,20},{5,21},{6,22},{7,23},{8,24},{9,... | collective-permute-start | bytes 442376 | tf_op jit(solution)/shard_map/ppermute | solution.py:559
  29.2 10.7 %collective-permute-start.4 = (bf16[2,4,48,384]{3,2,1,0:T(8,128)(2,1)S(1)}, bf16[2,4,48,384]{3,2,1,0:T(8,128)(2,1)S(1)}, u32[]{:S(2)}, u32[]{:S(2)}) collective-permute-start(bf16[2,4,48,384]{3,2,1,0:T(8,128)(2,1)S(1)} %get-tuple-element.168), channel_id=1, source_target_pairs={{0,12},{1,13},{2,14},{3,15},{4,8},{5,9},{6,10},{7,11},{8,4},{9,5},... | collective-permute-start | bytes 884744 | tf_op jit(solution)/shard_map/ppermute | solution.py:559
  32.8 11.8 %collective-permute-start.8 = (bf16[2,4,48,384]{3,2,1,0:T(8,128)(2,1)S(1)}, bf16[2,4,48,384]{3,2,1,0:T(8,128)(2,1)S(1)}, u32[]{:S(2)}, u32[]{:S(2)}) collective-permute-start(bf16[2,4,48,384]{3,2,1,0:T(8,128)(2,1)S(1)} %get-tuple-element.170), channel_id=1, source_target_pairs={{0,48},{1,49},{2,50},{3,51},{4,52},{5,53},{6,54},{7,55},{8,56},{9,... | collective-permute-start | bytes 884744 | tf_op jit(solution)/shard_map/ppermute | solution.py:559
  45.9 16.9 %collective-permute-start.9 = (bf16[4,2,4,48,384]{4,3,2,1,0:T(8,128)(2,1)}, bf16[4,2,4,48,384]{4,3,2,1,0:T(8,128)(2,1)}, u32[]{:S(2)}, u32[]{:S(2)}) collective-permute-start(bf16[4,2,4,48,384]{4,3,2,1,0:T(8,128)(2,1)} %get-tuple-element.156), channel_id=1, source_target_pairs={{0,1},{1,0},{2,3},{3,2},{4,5},{5,4},{6,7},{7,6},{8,9},{9,8},{10,11... | collective-permute-start | bytes 3538952 | tf_op jit(solution)/shard_map/ppermute | solution.py:559
  65.8 47.2 %collective-permute-start.13 = (bf16[2,4,2,4,48,384]{5,4,3,2,1,0:T(8,128)(2,1)}, bf16[2,4,2,4,48,384]{5,4,3,2,1,0:T(8,128)(2,1)}, u32[]{:S(2)}, u32[]{:S(2)}) collective-permute-start(bf16[2,4,2,4,48,384]{5,4,3,2,1,0:T(8,128)(2,1)} %pad_maximum_fusion.near), channel_id=1, source_target_pairs={{0,3},{1,2},{2,1},{3,0},{4,7},{5,6},{6,5},{7,4},{8,11},{9,10},{10,... | collective-permute-start | bytes 7077896 | tf_op jit(solution)/shard_map/ppermute | solution.py:559
  100.2 1.9 collective-permute-start.10
  106.3 1.9 collective-permute-start.11
  112.6 1.7 collective-permute-start.12
  123.3 1.6 collective-permute-start.14
  132.9 1.6 collective-permute-start.15
  143.5 1.6 collective-permute-start.16
  143.9 16.3 %collective-permute-start.18 = (bf16[208,768]{1,0:T(8,128)(2,1)S(1)}, bf16[208,768]{1,0:T(8,128)(2,1)}, u32[]{:S(2)}, u32[]{:S(2)}) collective-permute-start(bf16[208,768]{1,0:T(8,128)(2,1)S(1)} %get-tuple-element.119.mixed), channel_id=1, source_target_pairs={{0,64},{64,0},{1,65},{65,1},{2,66},{66,2},{3,67},{67,3},{4,68},{68... | collective-permute-start | bytes 958472 | tf_op jit(solution)/shard_map/ppermute | solution.py:546
  159.0 1.6 collective-permute-start.17
  166.6 16.3 %collective-permute-start.19 = (bf16[34,48,384]{2,1,0:T(8,128)(2,1)S(1)}, bf16[34,48,384]{2,1,0:T(8,128)(2,1)S(1)}, u32[]{:S(2)}, u32[]{:S(2)}) collective-permute-start(bf16[34,48,384]{2,1,0:T(8,128)(2,1)S(1)} %pad_maximum_fusion.2), channel_id=1, source_target_pairs={{0,3},{1,2},{2,1},{3,0},{4,7},{5,6},{6,5},{7,4},{8,11},{9,10},{10,... | collective-permute-start | bytes 3760136 | tf_op jit(solution)/shard_map/ppermute | solution.py:559
  183.3 10.8 %collective-permute-start.20 = (bf16[18,48,384]{2,1,0:T(8,128)(2,1)S(1)}, bf16[18,48,384]{2,1,0:T(8,128)(2,1)S(1)}, u32[]{:S(2)}, u32[]{:S(2)}) collective-permute-start(bf16[18,48,384]{2,1,0:T(8,128)(2,1)S(1)} %pad_maximum_fusion.6), channel_id=1, source_target_pairs={{0,1},{1,0},{2,3},{3,2},{4,5},{5,4},{6,7},{7,6},{8,9},{9,8},{10,11... | collective-permute-start | bytes 1990664 | tf_op jit(solution)/shard_map/ppermute | solution.py:559
  194.6 12.6 %collective-permute-start.21 = (bf16[10,48,384]{2,1,0:T(8,128)(2,1)S(1)}, bf16[10,48,384]{2,1,0:T(8,128)(2,1)S(1)}, u32[]{:S(2)}, u32[]{:S(2)}) collective-permute-start(bf16[10,48,384]{2,1,0:T(8,128)(2,1)S(1)} %pad_maximum_fusion.10), channel_id=1, source_target_pairs={{0,48},{1,49},{2,50},{3,51},{4,52},{5,53},{6,54},{7,55},{8,56},{9,... | collective-permute-start | bytes 1105928 | tf_op jit(solution)/shard_map/ppermute | solution.py:559
  207.3 6.1 %collective-permute-start.22 = (bf16[6,48,384]{2,1,0:T(8,128)(2,1)S(1)}, bf16[6,48,384]{2,1,0:T(8,128)(2,1)S(1)}, u32[]{:S(2)}, u32[]{:S(2)}) collective-permute-start(bf16[6,48,384]{2,1,0:T(8,128)(2,1)S(1)} %pad_maximum_fusion.13), channel_id=1, source_target_pairs={{0,16},{1,17},{2,18},{3,19},{4,20},{5,21},{6,22},{7,23},{8,24},{9,... | collective-permute-start | bytes 663560 | tf_op jit(solution)/shard_map/ppermute | solution.py:559
  209.4 7.0 %collective-permute-start.25 = (bf16[208,768]{1,0:T(8,128)(2,1)S(1)}, bf16[208,768]{1,0:T(8,128)(2,1)S(1)}, u32[]{:S(2)}, u32[]{:S(2)}) collective-permute-start(bf16[208,768]{1,0:T(8,128)(2,1)S(1)} %copy-done.25), channel_id=1, source_target_pairs={{0,1},{1,0},{2,3},{3,2},{4,5},{5,4},{6,7},{7,6},{8,9},{9,8},{10,11... | collective-permute-start | bytes 958472 | tf_op jit(solution)/shard_map/ppermute | solution.py:559
  213.5 4.1 %collective-permute-start.23 = (bf16[4,48,384]{2,1,0:T(8,128)(2,1)S(1)}, bf16[4,48,384]{2,1,0:T(8,128)(2,1)S(1)}, u32[]{:S(2)}, u32[]{:S(2)}) collective-permute-start(bf16[4,48,384]{2,1,0:T(8,128)(2,1)S(1)} %pad_maximum_fusion.16), channel_id=1, source_target_pairs={{0,12},{1,13},{2,14},{3,15},{4,8},{5,9},{6,10},{7,11},{8,4},{9,5},... | collective-permute-start | bytes 442376 | tf_op jit(solution)/shard_map/ppermute | solution.py:559
  216.5 9.7 %collective-permute-start.26 = (bf16[2,208,768]{2,1,0:T(8,128)(2,1)S(1)}, bf16[2,208,768]{2,1,0:T(8,128)(2,1)S(1)}, u32[]{:S(2)}, u32[]{:S(2)}) collective-permute-start(bf16[2,208,768]{2,1,0:T(8,128)(2,1)S(1)} %pad_maximum_fusion.7), channel_id=1, source_target_pairs={{0,3},{1,2},{2,1},{3,0},{4,7},{5,6},{6,5},{7,4},{8,11},{9,10},{10,... | collective-permute-start | bytes 1916936 | tf_op jit(solution)/shard_map/ppermute | solution.py:559
  217.6 8.2 %collective-permute-start.24 = (bf16[3,48,384]{2,1,0:T(8,128)(2,1)S(1)}, bf16[3,48,384]{2,1,0:T(8,128)(2,1)S(1)}, u32[]{:S(2)}, u32[]{:S(2)}) collective-permute-start(bf16[3,48,384]{2,1,0:T(8,128)(2,1)S(1)} %pad_maximum_fusion.18), channel_id=1, source_target_pairs={{0,4},{1,5},{2,6},{3,7},{4,0},{5,1},{6,2},{7,3},{8,12},{9,13},{10,... | collective-permute-start | bytes 331784 | tf_op jit(solution)/shard_map/ppermute | solution.py:559
  237.9 12.0 %collective-permute-start.27 = (bf16[48,8064]{1,0:T(8,128)(2,1)S(1)}, bf16[48,8064]{1,0:T(8,128)(2,1)S(1)}, u32[]{:S(2)}, u32[]{:S(2)}) collective-permute-start(bf16[48,8064]{1,0:T(8,128)(2,1)S(1)} %pad_maximum_fusion.5), channel_id=1, source_target_pairs={{0,1},{1,0},{2,3},{3,2},{4,5},{5,4},{6,7},{7,6},{8,9},{9,8},{10,11... | collective-permute-start | bytes 2322440 | tf_op jit(solution)/shard_map/ppermute | solution.py:559
  250.2 11.5 %collective-permute-start.28 = (bf16[48,8448]{1,0:T(8,128)(2,1)S(1)}, bf16[48,8448]{1,0:T(8,128)(2,1)S(1)}, u32[]{:S(2)}, u32[]{:S(2)}) collective-permute-start(bf16[48,8448]{1,0:T(8,128)(2,1)S(1)} %pad_maximum_fusion.4), channel_id=1, source_target_pairs={{0,3},{1,2},{2,1},{3,0},{4,7},{5,6},{6,5},{7,4},{8,11},{9,10},{10,... | collective-permute-start | bytes 2433032 | tf_op jit(solution)/shard_map/ppermute | solution.py:559
  262.7 5.0 %collective-permute-start.29 = (bf16[48,5376]{1,0:T(8,128)(2,1)S(1)}, bf16[48,5376]{1,0:T(8,128)(2,1)S(1)}, u32[]{:S(2)}, u32[]{:S(2)}) collective-permute-start(bf16[48,5376]{1,0:T(8,128)(2,1)S(1)} %broadcast_select_fusion.2), channel_id=1, source_target_pairs={{0,64},{64,0},{1,65},{65,1},{2,66},{66,2},{3,67},{67,3},{4,68},{68... | collective-permute-start | bytes 1548296 | tf_op jit(solution)/shard_map/ppermute | solution.py:546
  (38 other events, 384.3 us)
Sparse Core Ops, SparseCore 0:
  14.9 80.3 all-gather.3
  142.9 93.6 reduce-scatter.1
